TPU v7x, 512 devices: a whole 4x4x16 slice. The times are simulated.
512 devices in a mesh: lon: 32 (over x_hi, z), lat: 16 (over x_lo, y, core).
Axes of the slice: x: 4 (x_hi: 2, x_lo: 2; x = x_hi * 2 + x_lo), y: 4, z: 16, core: 2. Of those that a mesh axis runs over, the one named last changes fastest.
Arguments:
- fields: float32 [4, 10, 256, 4096], P(None, None, 'lat', 'lon'), may hold values from -4 to 4
- sea_mask: int32 [10, 256, 4096], P(None, 'lat', 'lon'), may hold values from 0 to 1, as said below
- bottom_level: int32 [256, 4096], P('lat', 'lon'), may hold values from 0 to 10, as said below
- coriolis: float32 [256, 4096], P('lat', 'lon'), may hold values from -1 to 1
Outputs:
- new_fields: float32 [4, 10, 256, 4096], P(None, None, 'lat', 'lon')
Inputs may be any that keep to these rules, and one draw needn't show every extreme that they name: sea_mask[k, y, x] is 1 exactly where k < bottom_level[y, x]. `bottom_level`: 0 marks a land column.
All inputs are finite; a program needn't handle non-finite values.
Results may differ from a plain program's by a relative error of at most 0.0003.
Values sent between devices are 32-bit elements; how exact they have to be, the bound alone decides.
No kernel may reach another device: no remote copies, remote signals or barrier semaphores. Data moves between devices by JAX's collectives and lax.ppermute only.
A program may use at most 64 MiB of HBM per device.

v0:
```python
import jax
import jax.numpy as jnp
from jax import lax
from jax.sharding import PartitionSpec as P

STEPS = 4


STEP_DT = 0.1
KAPPA = 0.2
DRAG_RATE = 0.5
GRAVITY = 0.1
ALPHA_T = 0.2
BETA_S = 0.15


def swapped(value, axis, apart):
    return lax.ppermute(value, axis, [(i, i ^ 1 << apart) for i in range(lax.axis_size(axis))])


def padded_2(block, sides, width, periodic):
    for axis, dim in sides:
        count = lax.axis_size(axis)
        forward = [(i, i + 1) for i in range(count - 1)]
        if periodic:
            forward.append((count - 1, 0))
        backward = [(target, source) for source, target in forward]
        low = lax.ppermute(
            lax.slice_in_dim(block, block.shape[dim] - width, None, axis=dim), axis, forward
        )
        high = lax.ppermute(lax.slice_in_dim(block, 0, width, axis=dim), axis, backward)
        block = jnp.concatenate([low, block, high], axis=dim)
    return block


def laplace(field, wetness):
    height = field.shape[-2]
    breadth = field.shape[-1]
    inside = field[..., 1:-1, 1:-1]
    wet_in = wetness[..., 1:-1, 1:-1]
    summed = jnp.zeros_like(inside)
    for shift_y, shift_x in ((0, 1), (2, 1), (1, 0), (1, 2)):
        beside = field[..., shift_y : shift_y + height - 2, shift_x : shift_x + breadth - 2]
        wet_beside = wetness[..., shift_y : shift_y + height - 2, shift_x : shift_x + breadth - 2]
        summed = summed + wet_in * wet_beside * (beside - inside)
    return summed


def advance(padded, wet_pad, pressure, coriolis, drag_on):
    center = padded[..., 2:-2, 2:-2]
    slope_east = 0.5 * (padded[..., 2:-2, 4:] - padded[..., 2:-2, :-4])
    slope_north = 0.5 * (padded[..., 4:, 2:-2] - padded[..., :-4, 2:-2])
    zonal_flow = center[2]
    merid_flow = center[3]
    carried = -(zonal_flow * slope_east + merid_flow * slope_north)
    first_pass = laplace(padded, wet_pad)
    smooth = laplace(first_pass, wet_pad[..., 1:-1, 1:-1])
    press_east = 0.5 * (pressure[..., 2:-2, 4:] - pressure[..., 2:-2, :-4])
    press_north = 0.5 * (pressure[..., 4:, 2:-2] - pressure[..., :-4, 2:-2])
    force_east = coriolis * merid_flow - press_east - DRAG_RATE * drag_on * zonal_flow
    force_north = -coriolis * zonal_flow - press_north - DRAG_RATE * drag_on * merid_flow
    nothing = jnp.zeros_like(force_east)
    forcing = jnp.stack([nothing, nothing, force_east, force_north])
    tendency = carried - KAPPA * smooth + forcing
    return wet_pad[..., 2:-2, 2:-2] * (center + STEP_DT * tendency)


def mirror_rows(top_rows):
    bit_count = lax.axis_size("lon").bit_length() - 1
    bit_order = list(range(bit_count))
    received = top_rows
    for bit_index in bit_order:
        received = swapped(received, "lon", bit_index)
    return received


def lat_extend(stacked, signs):
    padded = padded_2(stacked, (("lat", 2),), 2, False)
    partner_rows = mirror_rows(stacked[:, :, -2:, :])
    ghost = partner_rows[:, :, ::-1, ::-1] * signs[:, None, None, None]
    on_top = lax.axis_index("lat") == lax.axis_size("lat") - 1
    north = jnp.where(on_top, ghost, padded[:, :, -2:, :])
    return jnp.concatenate([padded[:, :, :-2, :], north], axis=2)


def lon_extend(stacked):
    return padded_2(stacked, (("lon", 3),), 2, True)


def extend(stacked, signs):
    return lon_extend(lat_extend(stacked, signs))


def local(fields, sea_mask, bottom_level, coriolis):
    wetness = sea_mask.astype(jnp.float32)
    wet_pad = extend(wetness[None], jnp.ones((1,), jnp.float32))[0]
    levels = sea_mask.shape[0]
    level_ids = lax.broadcasted_iota(jnp.int32, (levels, 1, 1), 0)
    drag_on = (level_ids == bottom_level[None] - 1).astype(jnp.float32)
    signs = jnp.array([1.0, 1.0, -1.0, -1.0], jnp.float32)
    state = fields
    for step_index in range(STEPS):
        padded = extend(state, signs)
        density = BETA_S * padded[1] - ALPHA_T * padded[0]
        pressure = GRAVITY * jnp.cumsum(density, axis=0)
        state = advance(padded, wet_pad, pressure, coriolis, drag_on)
    return state


def solution(mesh):
    in_specs = (
        P(None, None, "lat", "lon"),
        P(None, "lat", "lon"),
        P("lat", "lon"),
        P("lat", "lon"),
    )
    out_specs = P(None, None, "lat", "lon")
    return jax.shard_map(local, mesh=mesh, in_specs=in_specs, out_specs=out_specs, check_vma=False)
```

profile of v0, /device:TPU:24, one launch (start us, length us, event | category | flops | bytes accessed | tf_op | source)
XLA Modules:
  0.0 339.6 jit_solution(5251524740090858042)
XLA Ops:
  0.9 3.8 %collective-permute-start.1 = (f32[1,10,2,128]{3,2,1,0:T(2,128)S(1)}, f32[1,10,2,128]{3,2,1,0:T(2,128)S(1)}, u32[]{:S(2)}, u32[]{:S(2)}) collective-permute-start(f32[1,10,2,128]{3,2,1,0:T(2,128)S(1)} %get-tuple-element.49), channel_id=1, source_target_pairs={{0,16},{16,0},{32,48},{48,32},{64,80},{80,64},{96,112},{112,96},{1... | collective-permute-start | bytes 30728 | tf_op jit(solution)/shard_map/ppermute | solution.py:18
  5.8 2.0 collective-permute-start.10
  7.8 5.2 %collective-permute-start.2 = (f32[1,10,2,128]{3,2,1,0:T(2,128)S(1)}, f32[1,10,2,128]{3,2,1,0:T(2,128)S(1)}, u32[]{:S(2)}, u32[]{:S(2)}) collective-permute-start(f32[1,10,2,128]{3,2,1,0:T(2,128)S(1)} %collective-permute-done.1), channel_id=1, source_target_pairs={{0,32},{16,48},{32,0},{48,16},{64,96},{80,112},{96,64},{112,80},{1... | collective-permute-start | bytes 30728 | tf_op jit(solution)/shard_map/ppermute | solution.py:18
  14.7 9.1 %collective-permute-start.3 = (f32[1,10,2,128]{3,2,1,0:T(2,128)S(1)}, f32[1,10,2,128]{3,2,1,0:T(2,128)S(1)}, u32[]{:S(2)}, u32[]{:S(2)}) collective-permute-start(f32[1,10,2,128]{3,2,1,0:T(2,128)S(1)} %collective-permute-done.2), channel_id=1, source_target_pairs={{0,64},{16,80},{32,96},{48,112},{64,0},{80,16},{96,32},{112,48},{1... | collective-permute-start | bytes 30728 | tf_op jit(solution)/shard_map/ppermute | solution.py:18
  25.4 14.0 %collective-permute-start.4 = (f32[1,10,2,128]{3,2,1,0:T(2,128)S(1)}, f32[1,10,2,128]{3,2,1,0:T(2,128)S(1)}, u32[]{:S(2)}, u32[]{:S(2)}) collective-permute-start(f32[1,10,2,128]{3,2,1,0:T(2,128)S(1)} %collective-permute-done.3), channel_id=1, source_target_pairs={{0,128},{16,144},{32,160},{48,176},{64,192},{80,208},{96,224},{112... | collective-permute-start | bytes 30728 | tf_op jit(solution)/shard_map/ppermute | solution.py:18
  41.1 4.9 %collective-permute-start.5 = (f32[1,10,2,128]{3,2,1,0:T(2,128)S(1)}, f32[1,10,2,128]{3,2,1,0:T(2,128)S(1)}, u32[]{:S(2)}, u32[]{:S(2)}) collective-permute-start(f32[1,10,2,128]{3,2,1,0:T(2,128)S(1)} %collective-permute-done.4), channel_id=1, source_target_pairs={{0,256},{16,272},{32,288},{48,304},{64,320},{80,336},{96,352},{112... | collective-permute-start | bytes 30728 | tf_op jit(solution)/shard_map/ppermute | solution.py:18
  46.0 1.9 collective-permute-start.6
  47.9 2.4 collective-permute-start
  50.4 1.9 collective-permute-start.9
  52.3 3.6 %collective-permute-start.15 = (f32[4,10,2,128]{3,2,1,0:T(2,128)S(1)}, f32[4,10,2,128]{3,2,1,0:T(2,128)S(1)}, u32[]{:S(2)}, u32[]{:S(2)}) collective-permute-start(f32[4,10,2,128]{3,2,1,0:T(2,128)S(1)} %get-tuple-element.36), channel_id=1, source_target_pairs={{1,0},{2,1},{3,2},{4,3},{5,4},{6,5},{7,6},{8,7},{9,8},{10,9},{11,1... | collective-permute-start | bytes 122888 | tf_op jit(solution)/shard_map/ppermute | solution.py:31
  56.0 3.4 collective-permute-start.11
  59.7 3.8 %collective-permute-start.7 = (f32[1,10,20,2]{3,2,1,0:T(8,128)S(1)}, f32[1,10,20,2]{3,2,1,0:T(8,128)S(1)}, u32[]{:S(2)}, u32[]{:S(2)}) collective-permute-start(f32[1,10,20,2]{3,2,1,0:T(8,128)S(1)} %get-tuple-element.46), channel_id=1, source_target_pairs={{0,16},{16,32},{32,48},{48,64},{64,80},{80,96},{96,112},{112,128},... | collective-permute-start | bytes 4808 | tf_op jit(solution)/shard_map/ppermute | solution.py:28
  63.5 6.4 %collective-permute-start.8 = (f32[1,10,20,2]{3,2,1,0:T(8,128)S(1)}, f32[1,10,20,2]{3,2,1,0:T(8,128)S(1)}, u32[]{:S(2)}, u32[]{:S(2)}) collective-permute-start(f32[1,10,20,2]{3,2,1,0:T(8,128)S(1)} %get-tuple-element.47), channel_id=1, source_target_pairs={{16,0},{32,16},{48,32},{64,48},{80,64},{96,80},{112,96},{128,112},... | collective-permute-start | bytes 4808 | tf_op jit(solution)/shard_map/ppermute | solution.py:31
  69.8 4.7 %collective-permute-start.12 = (f32[4,10,2,128]{3,2,1,0:T(2,128)S(1)}, f32[4,10,2,128]{3,2,1,0:T(2,128)S(1)}, u32[]{:S(2)}, u32[]{:S(2)}) collective-permute-start(f32[4,10,2,128]{3,2,1,0:T(2,128)S(1)} %collective-permute-done.11), channel_id=1, source_target_pairs={{0,64},{16,80},{32,96},{48,112},{64,0},{80,16},{96,32},{112,48},{1... | collective-permute-start | bytes 122888 | tf_op jit(solution)/shard_map/ppermute | solution.py:18
  74.6 5.0 %collective-permute-done.12 = f32[4,10,2,128]{3,2,1,0:T(2,128)S(1)} collective-permute-done((f32[4,10,2,128]{3,2,1,0:T(2,128)S(1)}, f32[4,10,2,128]{3,2,1,0:T(2,128)S(1)}, u32[]{:S(2)}, u32[]{:S(2)}) %collective-permute-start.12) | collective-permute-done | bytes 40992 | tf_op jit(solution)/shard_map/ppermute | solution.py:18
  79.7 10.1 %collective-permute-start.13 = (f32[4,10,2,128]{3,2,1,0:T(2,128)S(1)}, f32[4,10,2,128]{3,2,1,0:T(2,128)S(1)}, u32[]{:S(2)}, u32[]{:S(2)}) collective-permute-start(f32[4,10,2,128]{3,2,1,0:T(2,128)S(1)} %collective-permute-done.12), channel_id=1, source_target_pairs={{0,128},{16,144},{32,160},{48,176},{64,192},{80,208},{96,224},{112... | collective-permute-start | bytes 122888 | tf_op jit(solution)/shard_map/ppermute | solution.py:18
  90.0 4.6 %collective-permute-done.13 = f32[4,10,2,128]{3,2,1,0:T(2,128)S(1)} collective-permute-done((f32[4,10,2,128]{3,2,1,0:T(2,128)S(1)}, f32[4,10,2,128]{3,2,1,0:T(2,128)S(1)}, u32[]{:S(2)}, u32[]{:S(2)}) %collective-permute-start.13) | collective-permute-done | bytes 40992 | tf_op jit(solution)/shard_map/ppermute | solution.py:18
  94.6 4.9 %collective-permute-start.14 = (f32[4,10,2,128]{3,2,1,0:T(2,128)S(1)}, f32[4,10,2,128]{3,2,1,0:T(2,128)S(1)}, u32[]{:S(2)}, u32[]{:S(2)}) collective-permute-start(f32[4,10,2,128]{3,2,1,0:T(2,128)S(1)} %collective-permute-done.13), channel_id=1, source_target_pairs={{0,256},{16,272},{32,288},{48,304},{64,320},{80,336},{96,352},{112... | collective-permute-start | bytes 122888 | tf_op jit(solution)/shard_map/ppermute | solution.py:18
  99.8 2.1 collective-permute-done.14
  102.6 1.9 collective-permute-start.17
  104.5 7.5 %collective-permute-start.16 = (f32[4,10,20,2]{3,2,1,0:T(8,128)S(1)}, f32[4,10,20,2]{3,2,1,0:T(8,128)S(1)}, u32[]{:S(2)}, u32[]{:S(2)}) collective-permute-start(f32[4,10,20,2]{3,2,1,0:T(8,128)S(1)} %get-tuple-element.20), channel_id=1, source_target_pairs={{16,0},{32,16},{48,32},{64,48},{80,64},{96,80},{112,96},{128,112},... | collective-permute-start | bytes 19208 | tf_op jit(solution)/shard_map/ppermute | solution.py:31
  112.2 5.3 %collective-permute-done.17 = f32[4,10,20,2]{3,2,1,0:T(8,128)S(1)} collective-permute-done((f32[4,10,20,2]{3,2,1,0:T(8,128)S(1)}, f32[4,10,20,2]{3,2,1,0:T(8,128)S(1)}, u32[]{:S(2)}, u32[]{:S(2)}) %collective-permute-start.17) | collective-permute-done | bytes 6432 | tf_op jit(solution)/shard_map/ppermute | solution.py:28
  121.8 1.9 collective-permute-start.19
  123.7 4.3 %collective-permute-done.19 = f32[4,10,2,128]{3,2,1,0:T(2,128)S(1)} collective-permute-done((f32[4,10,2,128]{3,2,1,0:T(2,128)S(1)}, f32[4,10,2,128]{3,2,1,0:T(2,128)S(1)}, u32[]{:S(2)}, u32[]{:S(2)}) %collective-permute-start.19) | collective-permute-done | bytes 40992 | tf_op jit(solution)/shard_map/ppermute | solution.py:18
  128.0 2.1 collective-permute-start.20
  130.1 4.7 %collective-permute-done.20 = f32[4,10,2,128]{3,2,1,0:T(2,128)S(1)} collective-permute-done((f32[4,10,2,128]{3,2,1,0:T(2,128)S(1)}, f32[4,10,2,128]{3,2,1,0:T(2,128)S(1)}, u32[]{:S(2)}, u32[]{:S(2)}) %collective-permute-start.20) | collective-permute-done | bytes 40992 | tf_op jit(solution)/shard_map/ppermute | solution.py:18
  134.8 4.2 %collective-permute-start.21 = (f32[4,10,2,128]{3,2,1,0:T(2,128)S(1)}, f32[4,10,2,128]{3,2,1,0:T(2,128)S(1)}, u32[]{:S(2)}, u32[]{:S(2)}) collective-permute-start(f32[4,10,2,128]{3,2,1,0:T(2,128)S(1)} %collective-permute-done.20), channel_id=1, source_target_pairs={{0,64},{16,80},{32,96},{48,112},{64,0},{80,16},{96,32},{112,48},{1... | collective-permute-start | bytes 122888 | tf_op jit(solution)/shard_map/ppermute | solution.py:18
  139.0 5.8 %collective-permute-done.21 = f32[4,10,2,128]{3,2,1,0:T(2,128)S(1)} collective-permute-done((f32[4,10,2,128]{3,2,1,0:T(2,128)S(1)}, f32[4,10,2,128]{3,2,1,0:T(2,128)S(1)}, u32[]{:S(2)}, u32[]{:S(2)}) %collective-permute-start.21) | collective-permute-done | bytes 40992 | tf_op jit(solution)/shard_map/ppermute | solution.py:18
  144.8 7.5 %collective-permute-start.22 = (f32[4,10,2,128]{3,2,1,0:T(2,128)S(1)}, f32[4,10,2,128]{3,2,1,0:T(2,128)S(1)}, u32[]{:S(2)}, u32[]{:S(2)}) collective-permute-start(f32[4,10,2,128]{3,2,1,0:T(2,128)S(1)} %collective-permute-done.21), channel_id=1, source_target_pairs={{0,128},{16,144},{32,160},{48,176},{64,192},{80,208},{96,224},{112... | collective-permute-start | bytes 122888 | tf_op jit(solution)/shard_map/ppermute | solution.py:18
  152.3 7.1 %collective-permute-done.22 = f32[4,10,2,128]{3,2,1,0:T(2,128)S(1)} collective-permute-done((f32[4,10,2,128]{3,2,1,0:T(2,128)S(1)}, f32[4,10,2,128]{3,2,1,0:T(2,128)S(1)}, u32[]{:S(2)}, u32[]{:S(2)}) %collective-permute-start.22) | collective-permute-done | bytes 40992 | tf_op jit(solution)/shard_map/ppermute | solution.py:18
  159.4 4.8 %collective-permute-start.23 = (f32[4,10,2,128]{3,2,1,0:T(2,128)S(1)}, f32[4,10,2,128]{3,2,1,0:T(2,128)S(1)}, u32[]{:S(2)}, u32[]{:S(2)}) collective-permute-start(f32[4,10,2,128]{3,2,1,0:T(2,128)S(1)} %collective-permute-done.22), channel_id=1, source_target_pairs={{0,256},{16,272},{32,288},{48,304},{64,320},{80,336},{96,352},{112... | collective-permute-start | bytes 122888 | tf_op jit(solution)/shard_map/ppermute | solution.py:18
  164.2 1.9 collective-permute-start.24
  166.1 2.4 collective-permute-start.18
  168.9 2.6 collective-permute-done.18
  171.7 2.1 collective-permute-start.26
  173.8 7.8 %collective-permute-start.25 = (f32[4,10,20,2]{3,2,1,0:T(8,128)S(1)}, f32[4,10,20,2]{3,2,1,0:T(8,128)S(1)}, u32[]{:S(2)}, u32[]{:S(2)}) collective-permute-start(f32[4,10,20,2]{3,2,1,0:T(8,128)S(1)} %get-tuple-element.18), channel_id=1, source_target_pairs={{16,0},{32,16},{48,32},{64,48},{80,64},{96,80},{112,96},{128,112},... | collective-permute-start | bytes 19208 | tf_op jit(solution)/shard_map/ppermute | solution.py:31
  181.6 9.2 %collective-permute-done.26 = f32[4,10,20,2]{3,2,1,0:T(8,128)S(1)} collective-permute-done((f32[4,10,20,2]{3,2,1,0:T(8,128)S(1)}, f32[4,10,20,2]{3,2,1,0:T(8,128)S(1)}, u32[]{:S(2)}, u32[]{:S(2)}) %collective-permute-start.26) | collective-permute-done | bytes 6432 | tf_op jit(solution)/shard_map/ppermute | solution.py:28
  195.7 1.9 collective-permute-start.28
  197.6 4.2 %collective-permute-done.28 = f32[4,10,2,128]{3,2,1,0:T(2,128)S(1)} collective-permute-done((f32[4,10,2,128]{3,2,1,0:T(2,128)S(1)}, f32[4,10,2,128]{3,2,1,0:T(2,128)S(1)}, u32[]{:S(2)}, u32[]{:S(2)}) %collective-permute-start.28) | collective-permute-done | bytes 40992 | tf_op jit(solution)/shard_map/ppermute | solution.py:18
  203.7 5.0 %collective-permute-done.29 = f32[4,10,2,128]{3,2,1,0:T(2,128)S(1)} collective-permute-done((f32[4,10,2,128]{3,2,1,0:T(2,128)S(1)}, f32[4,10,2,128]{3,2,1,0:T(2,128)S(1)}, u32[]{:S(2)}, u32[]{:S(2)}) %collective-permute-start.29) | collective-permute-done | bytes 40992 | tf_op jit(solution)/shard_map/ppermute | solution.py:18
  208.6 2.0 collective-permute-start.30
  210.7 8.2 %collective-permute-done.30 = f32[4,10,2,128]{3,2,1,0:T(2,128)S(1)} collective-permute-done((f32[4,10,2,128]{3,2,1,0:T(2,128)S(1)}, f32[4,10,2,128]{3,2,1,0:T(2,128)S(1)}, u32[]{:S(2)}, u32[]{:S(2)}) %collective-permute-start.30) | collective-permute-done | bytes 40992 | tf_op jit(solution)/shard_map/ppermute | solution.py:18
  218.9 3.6 %collective-permute-start.31 = (f32[4,10,2,128]{3,2,1,0:T(2,128)S(1)}, f32[4,10,2,128]{3,2,1,0:T(2,128)S(1)}, u32[]{:S(2)}, u32[]{:S(2)}) collective-permute-start(f32[4,10,2,128]{3,2,1,0:T(2,128)S(1)} %collective-permute-done.30), channel_id=1, source_target_pairs={{0,128},{16,144},{32,160},{48,176},{64,192},{80,208},{96,224},{112... | collective-permute-start | bytes 122888 | tf_op jit(solution)/shard_map/ppermute | solution.py:18
  222.5 11.0 %collective-permute-done.31 = f32[4,10,2,128]{3,2,1,0:T(2,128)S(1)} collective-permute-done((f32[4,10,2,128]{3,2,1,0:T(2,128)S(1)}, f32[4,10,2,128]{3,2,1,0:T(2,128)S(1)}, u32[]{:S(2)}, u32[]{:S(2)}) %collective-permute-start.31) | collective-permute-done | bytes 40992 | tf_op jit(solution)/shard_map/ppermute | solution.py:18
  233.5 2.9 collective-permute-start.32
  236.4 1.9 collective-permute-start.33
  238.3 2.4 collective-permute-start.27
  241.2 2.4 collective-permute-done.27
  243.9 2.6 collective-permute-start.35
  246.5 7.3 %collective-permute-start.34 = (f32[4,10,20,2]{3,2,1,0:T(8,128)S(1)}, f32[4,10,20,2]{3,2,1,0:T(8,128)S(1)}, u32[]{:S(2)}, u32[]{:S(2)}) collective-permute-start(f32[4,10,20,2]{3,2,1,0:T(8,128)S(1)} %get-tuple-element.16), channel_id=1, source_target_pairs={{16,0},{32,16},{48,32},{64,48},{80,64},{96,80},{112,96},{128,112},... | collective-permute-start | bytes 19208 | tf_op jit(solution)/shard_map/ppermute | solution.py:31
  253.9 8.4 %collective-permute-done.35 = f32[4,10,20,2]{3,2,1,0:T(8,128)S(1)} collective-permute-done((f32[4,10,20,2]{3,2,1,0:T(8,128)S(1)}, f32[4,10,20,2]{3,2,1,0:T(8,128)S(1)}, u32[]{:S(2)}, u32[]{:S(2)}) %collective-permute-start.35) | collective-permute-done | bytes 6432 | tf_op jit(solution)/shard_map/ppermute | solution.py:28
  266.6 1.9 collective-permute-start.37
  268.5 4.0 %collective-permute-done.37 = f32[4,10,2,128]{3,2,1,0:T(2,128)S(1)} collective-permute-done((f32[4,10,2,128]{3,2,1,0:T(2,128)S(1)}, f32[4,10,2,128]{3,2,1,0:T(2,128)S(1)}, u32[]{:S(2)}, u32[]{:S(2)}) %collective-permute-start.37) | collective-permute-done | bytes 40992 | tf_op jit(solution)/shard_map/ppermute | solution.py:18
  274.4 4.9 %collective-permute-done.38 = f32[4,10,2,128]{3,2,1,0:T(2,128)S(1)} collective-permute-done((f32[4,10,2,128]{3,2,1,0:T(2,128)S(1)}, f32[4,10,2,128]{3,2,1,0:T(2,128)S(1)}, u32[]{:S(2)}, u32[]{:S(2)}) %collective-permute-start.38) | collective-permute-done | bytes 40992 | tf_op jit(solution)/shard_map/ppermute | solution.py:18
  281.2 8.2 %collective-permute-done.39 = f32[4,10,2,128]{3,2,1,0:T(2,128)S(1)} collective-permute-done((f32[4,10,2,128]{3,2,1,0:T(2,128)S(1)}, f32[4,10,2,128]{3,2,1,0:T(2,128)S(1)}, u32[]{:S(2)}, u32[]{:S(2)}) %collective-permute-start.39) | collective-permute-done | bytes 40992 | tf_op jit(solution)/shard_map/ppermute | solution.py:18
  289.4 5.7 %collective-permute-start.40 = (f32[4,10,2,128]{3,2,1,0:T(2,128)S(1)}, f32[4,10,2,128]{3,2,1,0:T(2,128)S(1)}, u32[]{:S(2)}, u32[]{:S(2)}) collective-permute-start(f32[4,10,2,128]{3,2,1,0:T(2,128)S(1)} %collective-permute-done.39), channel_id=1, source_target_pairs={{0,128},{16,144},{32,160},{48,176},{64,192},{80,208},{96,224},{112... | collective-permute-start | bytes 122888 | tf_op jit(solution)/shard_map/ppermute | solution.py:18
  295.1 8.9 %collective-permute-done.40 = f32[4,10,2,128]{3,2,1,0:T(2,128)S(1)} collective-permute-done((f32[4,10,2,128]{3,2,1,0:T(2,128)S(1)}, f32[4,10,2,128]{3,2,1,0:T(2,128)S(1)}, u32[]{:S(2)}, u32[]{:S(2)}) %collective-permute-start.40) | collective-permute-done | bytes 40992 | tf_op jit(solution)/shard_map/ppermute | solution.py:18
  304.0 4.5 %collective-permute-start.41 = (f32[4,10,2,128]{3,2,1,0:T(2,128)S(1)}, f32[4,10,2,128]{3,2,1,0:T(2,128)S(1)}, u32[]{:S(2)}, u32[]{:S(2)}) collective-permute-start(f32[4,10,2,128]{3,2,1,0:T(2,128)S(1)} %collective-permute-done.40), channel_id=1, source_target_pairs={{0,256},{16,272},{32,288},{48,304},{64,320},{80,336},{96,352},{112... | collective-permute-start | bytes 122888 | tf_op jit(solution)/shard_map/ppermute | solution.py:18
  308.5 1.9 collective-permute-start.42
  310.4 2.4 collective-permute-start.36
  313.2 2.6 collective-permute-done.36
  316.0 2.1 collective-permute-start.44
  318.1 7.9 %collective-permute-start.43 = (f32[4,10,20,2]{3,2,1,0:T(8,128)S(1)}, f32[4,10,20,2]{3,2,1,0:T(8,128)S(1)}, u32[]{:S(2)}, u32[]{:S(2)}) collective-permute-start(f32[4,10,20,2]{3,2,1,0:T(8,128)S(1)} %get-tuple-element.14), channel_id=1, source_target_pairs={{16,0},{32,16},{48,32},{64,48},{80,64},{96,80},{112,96},{128,112},... | collective-permute-start | bytes 19208 | tf_op jit(solution)/shard_map/ppermute | solution.py:31
  326.0 8.7 %collective-permute-done.44 = f32[4,10,20,2]{3,2,1,0:T(8,128)S(1)} collective-permute-done((f32[4,10,20,2]{3,2,1,0:T(8,128)S(1)}, f32[4,10,20,2]{3,2,1,0:T(8,128)S(1)}, u32[]{:S(2)}, u32[]{:S(2)}) %collective-permute-start.44) | collective-permute-done | bytes 6432 | tf_op jit(solution)/shard_map/ppermute | solution.py:28
  (87 shorter events, 34.2 us)
Async XLA Ops:
  0.9 6.9 %collective-permute-start.1 = (f32[1,10,2,128]{3,2,1,0:T(2,128)S(1)}, f32[1,10,2,128]{3,2,1,0:T(2,128)S(1)}, u32[]{:S(2)}, u32[]{:S(2)}) collective-permute-start(f32[1,10,2,128]{3,2,1,0:T(2,128)S(1)} %get-tuple-element.49), channel_id=1, source_target_pairs={{0,16},{16,0},{32,48},{48,32},{64,80},{80,64},{96,112},{112,96},{1... | collective-permute-start | bytes 30728 | tf_op jit(solution)/shard_map/ppermute | solution.py:18
  5.8 46.5 %collective-permute-start.10 = (f32[4,10,2,128]{3,2,1,0:T(2,128)S(1)}, f32[4,10,2,128]{3,2,1,0:T(2,128)S(1)}, u32[]{:S(2)}, u32[]{:S(2)}) collective-permute-start(f32[4,10,2,128]{3,2,1,0:T(2,128)S(1)} %get-tuple-element.35), channel_id=1, source_target_pairs={{0,16},{16,0},{32,48},{48,32},{64,80},{80,64},{96,112},{112,96},{1... | collective-permute-start | bytes 122888 | tf_op jit(solution)/shard_map/ppermute | solution.py:18
  7.8 6.9 %collective-permute-start.2 = (f32[1,10,2,128]{3,2,1,0:T(2,128)S(1)}, f32[1,10,2,128]{3,2,1,0:T(2,128)S(1)}, u32[]{:S(2)}, u32[]{:S(2)}) collective-permute-start(f32[1,10,2,128]{3,2,1,0:T(2,128)S(1)} %collective-permute-done.1), channel_id=1, source_target_pairs={{0,32},{16,48},{32,0},{48,16},{64,96},{80,112},{96,64},{112,80},{1... | collective-permute-start | bytes 30728 | tf_op jit(solution)/shard_map/ppermute | solution.py:18
  14.7 10.8 %collective-permute-start.3 = (f32[1,10,2,128]{3,2,1,0:T(2,128)S(1)}, f32[1,10,2,128]{3,2,1,0:T(2,128)S(1)}, u32[]{:S(2)}, u32[]{:S(2)}) collective-permute-start(f32[1,10,2,128]{3,2,1,0:T(2,128)S(1)} %collective-permute-done.2), channel_id=1, source_target_pairs={{0,64},{16,80},{32,96},{48,112},{64,0},{80,16},{96,32},{112,48},{1... | collective-permute-start | bytes 30728 | tf_op jit(solution)/shard_map/ppermute | solution.py:18
  25.4 15.7 %collective-permute-start.4 = (f32[1,10,2,128]{3,2,1,0:T(2,128)S(1)}, f32[1,10,2,128]{3,2,1,0:T(2,128)S(1)}, u32[]{:S(2)}, u32[]{:S(2)}) collective-permute-start(f32[1,10,2,128]{3,2,1,0:T(2,128)S(1)} %collective-permute-done.3), channel_id=1, source_target_pairs={{0,128},{16,144},{32,160},{48,176},{64,192},{80,208},{96,224},{112... | collective-permute-start | bytes 30728 | tf_op jit(solution)/shard_map/ppermute | solution.py:18
  41.1 14.9 %collective-permute-start.5 = (f32[1,10,2,128]{3,2,1,0:T(2,128)S(1)}, f32[1,10,2,128]{3,2,1,0:T(2,128)S(1)}, u32[]{:S(2)}, u32[]{:S(2)}) collective-permute-start(f32[1,10,2,128]{3,2,1,0:T(2,128)S(1)} %collective-permute-done.4), channel_id=1, source_target_pairs={{0,256},{16,272},{32,288},{48,304},{64,320},{80,336},{96,352},{112... | collective-permute-start | bytes 30728 | tf_op jit(solution)/shard_map/ppermute | solution.py:18
  46.0 13.5 %collective-permute-start.6 = (f32[1,10,2,128]{3,2,1,0:T(2,128)S(1)}, f32[1,10,2,128]{3,2,1,0:T(2,128)S(1)}, u32[]{:S(2)}, u32[]{:S(2)}) collective-permute-start(f32[1,10,2,128]{3,2,1,0:T(2,128)S(1)} %get-tuple-element.48), channel_id=1, source_target_pairs={{1,0},{2,1},{3,2},{4,3},{5,4},{6,5},{7,6},{8,7},{9,8},{10,9},{11,1... | collective-permute-start | bytes 30728 | tf_op jit(solution)/shard_map/ppermute | solution.py:31
  47.9 11.6 %collective-permute-start = (f32[1,10,2,128]{3,2,1,0:T(2,128)S(1)}, f32[1,10,2,128]{3,2,1,0:T(2,128)S(1)}, u32[]{:S(2)}, u32[]{:S(2)}) collective-permute-start(f32[1,10,2,128]{3,2,1,0:T(2,128)S(1)} %get-tuple-element.49), channel_id=1, source_target_pairs={{0,1},{1,2},{2,3},{3,4},{4,5},{5,6},{6,7},{7,8},{8,9},{9,10},{10,1... | collective-permute-start | bytes 30728 | tf_op jit(solution)/shard_map/ppermute | solution.py:28
  50.4 51.9 %collective-permute-start.9 = (f32[4,10,2,128]{3,2,1,0:T(2,128)S(1)}, f32[4,10,2,128]{3,2,1,0:T(2,128)S(1)}, u32[]{:S(2)}, u32[]{:S(2)}) collective-permute-start(f32[4,10,2,128]{3,2,1,0:T(2,128)S(1)} %get-tuple-element.35), channel_id=1, source_target_pairs={{0,1},{1,2},{2,3},{3,4},{4,5},{5,6},{6,7},{7,8},{8,9},{9,10},{10,1... | collective-permute-start | bytes 122888 | tf_op jit(solution)/shard_map/ppermute | solution.py:28
  52.3 49.9 %collective-permute-start.15 = (f32[4,10,2,128]{3,2,1,0:T(2,128)S(1)}, f32[4,10,2,128]{3,2,1,0:T(2,128)S(1)}, u32[]{:S(2)}, u32[]{:S(2)}) collective-permute-start(f32[4,10,2,128]{3,2,1,0:T(2,128)S(1)} %get-tuple-element.36), channel_id=1, source_target_pairs={{1,0},{2,1},{3,2},{4,3},{5,4},{6,5},{7,6},{8,7},{9,8},{10,9},{11,1... | collective-permute-start | bytes 122888 | tf_op jit(solution)/shard_map/ppermute | solution.py:31
  56.0 13.9 %collective-permute-start.11 = (f32[4,10,2,128]{3,2,1,0:T(2,128)S(1)}, f32[4,10,2,128]{3,2,1,0:T(2,128)S(1)}, u32[]{:S(2)}, u32[]{:S(2)}) collective-permute-start(f32[4,10,2,128]{3,2,1,0:T(2,128)S(1)} %collective-permute-done.10), channel_id=1, source_target_pairs={{0,32},{16,48},{32,0},{48,16},{64,96},{80,112},{96,64},{112,80},{1... | collective-permute-start | bytes 122888 | tf_op jit(solution)/shard_map/ppermute | solution.py:18
  59.5 15.0 %copy-start.3 = (s32[16,128]{1,0:T(8,128)S(1)}, s32[16,128]{1,0:T(8,128)}, u32[]{:S(2)}) copy-start(s32[16,128]{1,0:T(8,128)} %param.7) | copy-start | bytes 24580
  59.7 30.1 %collective-permute-start.7 = (f32[1,10,20,2]{3,2,1,0:T(8,128)S(1)}, f32[1,10,20,2]{3,2,1,0:T(8,128)S(1)}, u32[]{:S(2)}, u32[]{:S(2)}) collective-permute-start(f32[1,10,20,2]{3,2,1,0:T(8,128)S(1)} %get-tuple-element.46), channel_id=1, source_target_pairs={{0,16},{16,32},{32,48},{48,64},{64,80},{80,96},{96,112},{112,128},... | collective-permute-start | bytes 4808 | tf_op jit(solution)/shard_map/ppermute | solution.py:28
  63.5 11.1 %copy-start.1 = (f32[16,128]{1,0:T(8,128)S(1)}, f32[16,128]{1,0:T(8,128)}, u32[]{:S(2)}) copy-start(f32[16,128]{1,0:T(8,128)} %param.8) | copy-start | bytes 24580
  63.5 26.3 %collective-permute-start.8 = (f32[1,10,20,2]{3,2,1,0:T(8,128)S(1)}, f32[1,10,20,2]{3,2,1,0:T(8,128)S(1)}, u32[]{:S(2)}, u32[]{:S(2)}) collective-permute-start(f32[1,10,20,2]{3,2,1,0:T(8,128)S(1)} %get-tuple-element.47), channel_id=1, source_target_pairs={{16,0},{32,16},{48,32},{64,48},{80,64},{96,80},{112,96},{128,112},... | collective-permute-start | bytes 4808 | tf_op jit(solution)/shard_map/ppermute | solution.py:31
  69.8 9.8 %collective-permute-start.12 = (f32[4,10,2,128]{3,2,1,0:T(2,128)S(1)}, f32[4,10,2,128]{3,2,1,0:T(2,128)S(1)}, u32[]{:S(2)}, u32[]{:S(2)}) collective-permute-start(f32[4,10,2,128]{3,2,1,0:T(2,128)S(1)} %collective-permute-done.11), channel_id=1, source_target_pairs={{0,64},{16,80},{32,96},{48,112},{64,0},{80,16},{96,32},{112,48},{1... | collective-permute-start | bytes 122888 | tf_op jit(solution)/shard_map/ppermute | solution.py:18
  79.7 14.9 %collective-permute-start.13 = (f32[4,10,2,128]{3,2,1,0:T(2,128)S(1)}, f32[4,10,2,128]{3,2,1,0:T(2,128)S(1)}, u32[]{:S(2)}, u32[]{:S(2)}) collective-permute-start(f32[4,10,2,128]{3,2,1,0:T(2,128)S(1)} %collective-permute-done.12), channel_id=1, source_target_pairs={{0,128},{16,144},{32,160},{48,176},{64,192},{80,208},{96,224},{112... | collective-permute-start | bytes 122888 | tf_op jit(solution)/shard_map/ppermute | solution.py:18
  94.6 7.4 %collective-permute-start.14 = (f32[4,10,2,128]{3,2,1,0:T(2,128)S(1)}, f32[4,10,2,128]{3,2,1,0:T(2,128)S(1)}, u32[]{:S(2)}, u32[]{:S(2)}) collective-permute-start(f32[4,10,2,128]{3,2,1,0:T(2,128)S(1)} %collective-permute-done.13), channel_id=1, source_target_pairs={{0,256},{16,272},{32,288},{48,304},{64,320},{80,336},{96,352},{112... | collective-permute-start | bytes 122888 | tf_op jit(solution)/shard_map/ppermute | solution.py:18
  99.5 2.8 copy-start
  99.8 2.4 copy-start.2
  102.6 15.0 %collective-permute-start.17 = (f32[4,10,20,2]{3,2,1,0:T(8,128)S(1)}, f32[4,10,20,2]{3,2,1,0:T(8,128)S(1)}, u32[]{:S(2)}, u32[]{:S(2)}) collective-permute-start(f32[4,10,20,2]{3,2,1,0:T(8,128)S(1)} %get-tuple-element.19), channel_id=1, source_target_pairs={{0,16},{16,32},{32,48},{48,64},{64,80},{80,96},{96,112},{112,128},... | collective-permute-start | bytes 19208 | tf_op jit(solution)/shard_map/ppermute | solution.py:28
  104.5 14.2 %collective-permute-start.16 = (f32[4,10,20,2]{3,2,1,0:T(8,128)S(1)}, f32[4,10,20,2]{3,2,1,0:T(8,128)S(1)}, u32[]{:S(2)}, u32[]{:S(2)}) collective-permute-start(f32[4,10,20,2]{3,2,1,0:T(8,128)S(1)} %get-tuple-element.20), channel_id=1, source_target_pairs={{16,0},{32,16},{48,32},{64,48},{80,64},{96,80},{112,96},{128,112},... | collective-permute-start | bytes 19208 | tf_op jit(solution)/shard_map/ppermute | solution.py:31
  121.8 6.2 %collective-permute-start.19 = (f32[4,10,2,128]{3,2,1,0:T(2,128)S(1)}, f32[4,10,2,128]{3,2,1,0:T(2,128)S(1)}, u32[]{:S(2)}, u32[]{:S(2)}) collective-permute-start(f32[4,10,2,128]{3,2,1,0:T(2,128)S(1)} %get-tuple-element.31), channel_id=1, source_target_pairs={{0,16},{16,0},{32,48},{48,32},{64,80},{80,64},{96,112},{112,96},{1... | collective-permute-start | bytes 122888 | tf_op jit(solution)/shard_map/ppermute | solution.py:18
  128.0 6.8 %collective-permute-start.20 = (f32[4,10,2,128]{3,2,1,0:T(2,128)S(1)}, f32[4,10,2,128]{3,2,1,0:T(2,128)S(1)}, u32[]{:S(2)}, u32[]{:S(2)}) collective-permute-start(f32[4,10,2,128]{3,2,1,0:T(2,128)S(1)} %collective-permute-done.19), channel_id=1, source_target_pairs={{0,32},{16,48},{32,0},{48,16},{64,96},{80,112},{96,64},{112,80},{1... | collective-permute-start | bytes 122888 | tf_op jit(solution)/shard_map/ppermute | solution.py:18
  134.8 10.0 %collective-permute-start.21 = (f32[4,10,2,128]{3,2,1,0:T(2,128)S(1)}, f32[4,10,2,128]{3,2,1,0:T(2,128)S(1)}, u32[]{:S(2)}, u32[]{:S(2)}) collective-permute-start(f32[4,10,2,128]{3,2,1,0:T(2,128)S(1)} %collective-permute-done.20), channel_id=1, source_target_pairs={{0,64},{16,80},{32,96},{48,112},{64,0},{80,16},{96,32},{112,48},{1... | collective-permute-start | bytes 122888 | tf_op jit(solution)/shard_map/ppermute | solution.py:18
  144.8 14.6 %collective-permute-start.22 = (f32[4,10,2,128]{3,2,1,0:T(2,128)S(1)}, f32[4,10,2,128]{3,2,1,0:T(2,128)S(1)}, u32[]{:S(2)}, u32[]{:S(2)}) collective-permute-start(f32[4,10,2,128]{3,2,1,0:T(2,128)S(1)} %collective-permute-done.21), channel_id=1, source_target_pairs={{0,128},{16,144},{32,160},{48,176},{64,192},{80,208},{96,224},{112... | collective-permute-start | bytes 122888 | tf_op jit(solution)/shard_map/ppermute | solution.py:18
  159.4 9.1 %collective-permute-start.23 = (f32[4,10,2,128]{3,2,1,0:T(2,128)S(1)}, f32[4,10,2,128]{3,2,1,0:T(2,128)S(1)}, u32[]{:S(2)}, u32[]{:S(2)}) collective-permute-start(f32[4,10,2,128]{3,2,1,0:T(2,128)S(1)} %collective-permute-done.22), channel_id=1, source_target_pairs={{0,256},{16,272},{32,288},{48,304},{64,320},{80,336},{96,352},{112... | collective-permute-start | bytes 122888 | tf_op jit(solution)/shard_map/ppermute | solution.py:18
  164.2 4.6 %collective-permute-start.24 = (f32[4,10,2,128]{3,2,1,0:T(2,128)S(1)}, f32[4,10,2,128]{3,2,1,0:T(2,128)S(1)}, u32[]{:S(2)}, u32[]{:S(2)}) collective-permute-start(f32[4,10,2,128]{3,2,1,0:T(2,128)S(1)} %get-tuple-element.32), channel_id=1, source_target_pairs={{1,0},{2,1},{3,2},{4,3},{5,4},{6,5},{7,6},{8,7},{9,8},{10,9},{11,1... | collective-permute-start | bytes 122888 | tf_op jit(solution)/shard_map/ppermute | solution.py:31
  166.1 5.3 %collective-permute-start.18 = (f32[4,10,2,128]{3,2,1,0:T(2,128)S(1)}, f32[4,10,2,128]{3,2,1,0:T(2,128)S(1)}, u32[]{:S(2)}, u32[]{:S(2)}) collective-permute-start(f32[4,10,2,128]{3,2,1,0:T(2,128)S(1)} %get-tuple-element.31), channel_id=1, source_target_pairs={{0,1},{1,2},{2,3},{3,4},{4,5},{5,6},{6,7},{7,8},{8,9},{9,10},{10,1... | collective-permute-start | bytes 122888 | tf_op jit(solution)/shard_map/ppermute | solution.py:28
  171.7 19.1 %collective-permute-start.26 = (f32[4,10,20,2]{3,2,1,0:T(8,128)S(1)}, f32[4,10,20,2]{3,2,1,0:T(8,128)S(1)}, u32[]{:S(2)}, u32[]{:S(2)}) collective-permute-start(f32[4,10,20,2]{3,2,1,0:T(8,128)S(1)} %get-tuple-element.17), channel_id=1, source_target_pairs={{0,16},{16,32},{32,48},{48,64},{64,80},{80,96},{96,112},{112,128},... | collective-permute-start | bytes 19208 | tf_op jit(solution)/shard_map/ppermute | solution.py:28
  173.8 18.8 %collective-permute-start.25 = (f32[4,10,20,2]{3,2,1,0:T(8,128)S(1)}, f32[4,10,20,2]{3,2,1,0:T(8,128)S(1)}, u32[]{:S(2)}, u32[]{:S(2)}) collective-permute-start(f32[4,10,20,2]{3,2,1,0:T(8,128)S(1)} %get-tuple-element.18), channel_id=1, source_target_pairs={{16,0},{32,16},{48,32},{64,48},{80,64},{96,80},{112,96},{128,112},... | collective-permute-start | bytes 19208 | tf_op jit(solution)/shard_map/ppermute | solution.py:31
  195.7 6.1 %collective-permute-start.28 = (f32[4,10,2,128]{3,2,1,0:T(2,128)S(1)}, f32[4,10,2,128]{3,2,1,0:T(2,128)S(1)}, u32[]{:S(2)}, u32[]{:S(2)}) collective-permute-start(f32[4,10,2,128]{3,2,1,0:T(2,128)S(1)} %get-tuple-element.27), channel_id=1, source_target_pairs={{0,16},{16,0},{32,48},{48,32},{64,80},{80,64},{96,112},{112,96},{1... | collective-permute-start | bytes 122888 | tf_op jit(solution)/shard_map/ppermute | solution.py:18
  201.8 6.9 %collective-permute-start.29 = (f32[4,10,2,128]{3,2,1,0:T(2,128)S(1)}, f32[4,10,2,128]{3,2,1,0:T(2,128)S(1)}, u32[]{:S(2)}, u32[]{:S(2)}) collective-permute-start(f32[4,10,2,128]{3,2,1,0:T(2,128)S(1)} %collective-permute-done.28), channel_id=1, source_target_pairs={{0,32},{16,48},{32,0},{48,16},{64,96},{80,112},{96,64},{112,80},{1... | collective-permute-start | bytes 122888 | tf_op jit(solution)/shard_map/ppermute | solution.py:18
  208.6 10.3 %collective-permute-start.30 = (f32[4,10,2,128]{3,2,1,0:T(2,128)S(1)}, f32[4,10,2,128]{3,2,1,0:T(2,128)S(1)}, u32[]{:S(2)}, u32[]{:S(2)}) collective-permute-start(f32[4,10,2,128]{3,2,1,0:T(2,128)S(1)} %collective-permute-done.29), channel_id=1, source_target_pairs={{0,64},{16,80},{32,96},{48,112},{64,0},{80,16},{96,32},{112,48},{1... | collective-permute-start | bytes 122888 | tf_op jit(solution)/shard_map/ppermute | solution.py:18
  218.9 14.6 %collective-permute-start.31 = (f32[4,10,2,128]{3,2,1,0:T(2,128)S(1)}, f32[4,10,2,128]{3,2,1,0:T(2,128)S(1)}, u32[]{:S(2)}, u32[]{:S(2)}) collective-permute-start(f32[4,10,2,128]{3,2,1,0:T(2,128)S(1)} %collective-permute-done.30), channel_id=1, source_target_pairs={{0,128},{16,144},{32,160},{48,176},{64,192},{80,208},{96,224},{112... | collective-permute-start | bytes 122888 | tf_op jit(solution)/shard_map/ppermute | solution.py:18
  233.5 7.4 %collective-permute-start.32 = (f32[4,10,2,128]{3,2,1,0:T(2,128)S(1)}, f32[4,10,2,128]{3,2,1,0:T(2,128)S(1)}, u32[]{:S(2)}, u32[]{:S(2)}) collective-permute-start(f32[4,10,2,128]{3,2,1,0:T(2,128)S(1)} %collective-permute-done.31), channel_id=1, source_target_pairs={{0,256},{16,272},{32,288},{48,304},{64,320},{80,336},{96,352},{112... | collective-permute-start | bytes 122888 | tf_op jit(solution)/shard_map/ppermute | solution.py:18
  236.4 4.7 %collective-permute-start.33 = (f32[4,10,2,128]{3,2,1,0:T(2,128)S(1)}, f32[4,10,2,128]{3,2,1,0:T(2,128)S(1)}, u32[]{:S(2)}, u32[]{:S(2)}) collective-permute-start(f32[4,10,2,128]{3,2,1,0:T(2,128)S(1)} %get-tuple-element.28), channel_id=1, source_target_pairs={{1,0},{2,1},{3,2},{4,3},{5,4},{6,5},{7,6},{8,7},{9,8},{10,9},{11,1... | collective-permute-start | bytes 122888 | tf_op jit(solution)/shard_map/ppermute | solution.py:31
  238.3 5.3 %collective-permute-start.27 = (f32[4,10,2,128]{3,2,1,0:T(2,128)S(1)}, f32[4,10,2,128]{3,2,1,0:T(2,128)S(1)}, u32[]{:S(2)}, u32[]{:S(2)}) collective-permute-start(f32[4,10,2,128]{3,2,1,0:T(2,128)S(1)} %get-tuple-element.27), channel_id=1, source_target_pairs={{0,1},{1,2},{2,3},{3,4},{4,5},{5,6},{6,7},{7,8},{8,9},{9,10},{10,1... | collective-permute-start | bytes 122888 | tf_op jit(solution)/shard_map/ppermute | solution.py:28
  243.9 18.4 %collective-permute-start.35 = (f32[4,10,20,2]{3,2,1,0:T(8,128)S(1)}, f32[4,10,20,2]{3,2,1,0:T(8,128)S(1)}, u32[]{:S(2)}, u32[]{:S(2)}) collective-permute-start(f32[4,10,20,2]{3,2,1,0:T(8,128)S(1)} %get-tuple-element.15), channel_id=1, source_target_pairs={{0,16},{16,32},{32,48},{48,64},{64,80},{80,96},{96,112},{112,128},... | collective-permute-start | bytes 19208 | tf_op jit(solution)/shard_map/ppermute | solution.py:28
  246.5 17.0 %collective-permute-start.34 = (f32[4,10,20,2]{3,2,1,0:T(8,128)S(1)}, f32[4,10,20,2]{3,2,1,0:T(8,128)S(1)}, u32[]{:S(2)}, u32[]{:S(2)}) collective-permute-start(f32[4,10,20,2]{3,2,1,0:T(8,128)S(1)} %get-tuple-element.16), channel_id=1, source_target_pairs={{16,0},{32,16},{48,32},{64,48},{80,64},{96,80},{112,96},{128,112},... | collective-permute-start | bytes 19208 | tf_op jit(solution)/shard_map/ppermute | solution.py:31
  266.6 5.9 %collective-permute-start.37 = (f32[4,10,2,128]{3,2,1,0:T(2,128)S(1)}, f32[4,10,2,128]{3,2,1,0:T(2,128)S(1)}, u32[]{:S(2)}, u32[]{:S(2)}) collective-permute-start(f32[4,10,2,128]{3,2,1,0:T(2,128)S(1)} %get-tuple-element.23), channel_id=1, source_target_pairs={{0,16},{16,0},{32,48},{48,32},{64,80},{80,64},{96,112},{112,96},{1... | collective-permute-start | bytes 122888 | tf_op jit(solution)/shard_map/ppermute | solution.py:18
  272.5 6.8 %collective-permute-start.38 = (f32[4,10,2,128]{3,2,1,0:T(2,128)S(1)}, f32[4,10,2,128]{3,2,1,0:T(2,128)S(1)}, u32[]{:S(2)}, u32[]{:S(2)}) collective-permute-start(f32[4,10,2,128]{3,2,1,0:T(2,128)S(1)} %collective-permute-done.37), channel_id=1, source_target_pairs={{0,32},{16,48},{32,0},{48,16},{64,96},{80,112},{96,64},{112,80},{1... | collective-permute-start | bytes 122888 | tf_op jit(solution)/shard_map/ppermute | solution.py:18
  279.2 10.1 %collective-permute-start.39 = (f32[4,10,2,128]{3,2,1,0:T(2,128)S(1)}, f32[4,10,2,128]{3,2,1,0:T(2,128)S(1)}, u32[]{:S(2)}, u32[]{:S(2)}) collective-permute-start(f32[4,10,2,128]{3,2,1,0:T(2,128)S(1)} %collective-permute-done.38), channel_id=1, source_target_pairs={{0,64},{16,80},{32,96},{48,112},{64,0},{80,16},{96,32},{112,48},{1... | collective-permute-start | bytes 122888 | tf_op jit(solution)/shard_map/ppermute | solution.py:18
  289.4 14.6 %collective-permute-start.40 = (f32[4,10,2,128]{3,2,1,0:T(2,128)S(1)}, f32[4,10,2,128]{3,2,1,0:T(2,128)S(1)}, u32[]{:S(2)}, u32[]{:S(2)}) collective-permute-start(f32[4,10,2,128]{3,2,1,0:T(2,128)S(1)} %collective-permute-done.39), channel_id=1, source_target_pairs={{0,128},{16,144},{32,160},{48,176},{64,192},{80,208},{96,224},{112... | collective-permute-start | bytes 122888 | tf_op jit(solution)/shard_map/ppermute | solution.py:18
  304.0 8.9 %collective-permute-start.41 = (f32[4,10,2,128]{3,2,1,0:T(2,128)S(1)}, f32[4,10,2,128]{3,2,1,0:T(2,128)S(1)}, u32[]{:S(2)}, u32[]{:S(2)}) collective-permute-start(f32[4,10,2,128]{3,2,1,0:T(2,128)S(1)} %collective-permute-done.40), channel_id=1, source_target_pairs={{0,256},{16,272},{32,288},{48,304},{64,320},{80,336},{96,352},{112... | collective-permute-start | bytes 122888 | tf_op jit(solution)/shard_map/ppermute | solution.py:18
  308.5 4.6 %collective-permute-start.42 = (f32[4,10,2,128]{3,2,1,0:T(2,128)S(1)}, f32[4,10,2,128]{3,2,1,0:T(2,128)S(1)}, u32[]{:S(2)}, u32[]{:S(2)}) collective-permute-start(f32[4,10,2,128]{3,2,1,0:T(2,128)S(1)} %get-tuple-element.24), channel_id=1, source_target_pairs={{1,0},{2,1},{3,2},{4,3},{5,4},{6,5},{7,6},{8,7},{9,8},{10,9},{11,1... | collective-permute-start | bytes 122888 | tf_op jit(solution)/shard_map/ppermute | solution.py:31
  310.4 5.3 %collective-permute-start.36 = (f32[4,10,2,128]{3,2,1,0:T(2,128)S(1)}, f32[4,10,2,128]{3,2,1,0:T(2,128)S(1)}, u32[]{:S(2)}, u32[]{:S(2)}) collective-permute-start(f32[4,10,2,128]{3,2,1,0:T(2,128)S(1)} %get-tuple-element.23), channel_id=1, source_target_pairs={{0,1},{1,2},{2,3},{3,4},{4,5},{5,6},{6,7},{7,8},{8,9},{9,10},{10,1... | collective-permute-start | bytes 122888 | tf_op jit(solution)/shard_map/ppermute | solution.py:28
  316.0 18.7 %collective-permute-start.44 = (f32[4,10,20,2]{3,2,1,0:T(8,128)S(1)}, f32[4,10,20,2]{3,2,1,0:T(8,128)S(1)}, u32[]{:S(2)}, u32[]{:S(2)}) collective-permute-start(f32[4,10,20,2]{3,2,1,0:T(8,128)S(1)} %get-tuple-element.13), channel_id=1, source_target_pairs={{0,16},{16,32},{32,48},{48,64},{64,80},{80,96},{96,112},{112,128},... | collective-permute-start | bytes 19208 | tf_op jit(solution)/shard_map/ppermute | solution.py:28
  318.1 17.8 %collective-permute-start.43 = (f32[4,10,20,2]{3,2,1,0:T(8,128)S(1)}, f32[4,10,20,2]{3,2,1,0:T(8,128)S(1)}, u32[]{:S(2)}, u32[]{:S(2)}) collective-permute-start(f32[4,10,20,2]{3,2,1,0:T(8,128)S(1)} %get-tuple-element.14), channel_id=1, source_target_pairs={{16,0},{32,16},{48,32},{64,48},{80,64},{96,80},{112,96},{128,112},... | collective-permute-start | bytes 19208 | tf_op jit(solution)/shard_map/ppermute | solution.py:31
where the time goes:
time: 341 us; the launch traced here: 340 us
  starting transfers between devices  183 us (54%)
  waiting for transfers between devices  138 us (40%)
  other arithmetic  14.9 us (4%)
    ppermute x25, starting transfers between devices, swapped(): lax.ppermute(value, axis, [(i, i ^ 1 << apart) for i in range(lax.axis_si...  111 us
    ppermute x25, waiting for transfers between devices, swapped(): lax.ppermute(value, axis, [(i, i ^ 1 << apart) for i in range(lax.axis_si...  93.1 us
    ppermute x10, starting transfers between devices, padded_2(): lax.ppermute(lax.slice_in_dim(block, 0, width, axis=dim), axis, backward)  48.2 us
    ppermute x10, waiting for transfers between devices, padded_2(): lax.ppermute(lax.slice_in_dim(block, block.shape[dim] - width, None, axis...  39.3 us
    ppermute x10, starting transfers between devices, padded_2(): lax.ppermute(lax.slice_in_dim(block, block.shape[dim] - width, None, axis...  24.1 us
  transfers between devices with their start and end apart: 45, of which 30 were waited for; matrix products, arithmetic and copies ran while one was open for 1% of the time, Pallas kernels for 0%

commit v1 on v0

v1 whole, which is shorter than its diff:
```python
import functools

import jax
import jax.numpy as jnp
from jax import lax
from jax.experimental import pallas as pl
from jax.experimental.pallas import tpu as pltpu
from jax.sharding import PartitionSpec as P

STEPS = 4
STEP_DT = 0.1
KAPPA = 0.2
DRAG_RATE = 0.5
GRAVITY = 0.1
ALPHA_T = 0.2
BETA_S = 0.15

COMPS = 4
LEVELS = 10
PAIRS = LEVELS // 2
SLABS = LEVELS + PAIRS
PLANES = COMPS * LEVELS + 2
ROWS = 16
HALO = 8
EXT = ROWS + 2 * HALO
PITCH = EXT + 16
LANES = 128
GROUPS = 3


def lane_ids(rows):
    return lax.broadcasted_iota(jnp.int32, (rows, LANES), 1)


def turned(by):
    if by % LANES == 0:
        return lambda value: value
    return lambda value: pltpu.roll(value, by % LANES, 1)


def beside(value):
    return turned(-1)(value + turned(2)(value))


def sloped(value):
    return turned(-2)(value) - turned(2)(value)


def beside_and_sloped(value):
    two_west = turned(2)(value)
    return turned(-1)(value + two_west), turned(-2)(value) - two_west


def pack_lat_kernel(lat_ref, fields_ref, bottom_ref, coriolis_ref, first_ref, second_ref, *, lat_count):
    lat = lat_ref[0]
    even = lat % 2 == 0
    first_row = pl.multiple_of(jnp.where(even, HALO, 0), HALO)
    second_row = pl.multiple_of(jnp.where(even, 0, HALO), HALO)

    def copied(row, out_ref):
        for comp in range(COMPS):
            for level in range(LEVELS):
                out_ref[comp * LEVELS + level] = fields_ref[comp, level, pl.ds(row, HALO), :]
        out_ref[PLANES - 2] = bottom_ref[pl.ds(row, HALO), :].astype(jnp.float32)
        out_ref[PLANES - 1] = coriolis_ref[pl.ds(row, HALO), :]

    copied(first_row, first_ref)
    copied(second_row, second_ref)

    @pl.when(lat == lat_count - 1)
    def _():
        lanes = LANES - 1 - lane_ids(HALO)
        rows = HALO - 1 - lax.broadcasted_iota(jnp.int32, (HALO, LANES), 0)
        for plane in range(PLANES):
            value = second_ref[plane]
            value = jnp.take_along_axis(value, lanes, axis=1)
            value = jnp.take_along_axis(value, rows, axis=0)
            if 2 * LEVELS <= plane < 4 * LEVELS:
                value = -value
            second_ref[plane] = value


def extended(plane, own, first, second, even):
    one, two = first[plane], second[plane]
    south = jnp.where(even, two, one)
    north = jnp.where(even, one, two)
    return south, own, north


def pack_lon_kernel(lat_ref, fields_ref, bottom_ref, coriolis_ref, first_ref, second_ref, west_ref, east_ref):
    even = lat_ref[0] % 2 == 0
    lanes = lane_ids(EXT)

    def ext(plane, own):
        return jnp.concatenate(extended(plane, own, first_ref, second_ref, even), axis=0)

    def pair(index):
        if index < COMPS * PAIRS:
            comp, level = divmod(index, PAIRS)
            return (
                ext(comp * LEVELS + level, fields_ref[comp, level]),
                ext(comp * LEVELS + level + PAIRS, fields_ref[comp, level + PAIRS]),
            )
        if index == COMPS * PAIRS:
            value = ext(PLANES - 2, bottom_ref[...].astype(jnp.float32))
        else:
            value = ext(PLANES - 1, coriolis_ref[...])
        return value, value

    for group in range(GROUPS):
        west = jnp.zeros((EXT, LANES), jnp.float32)
        east = jnp.zeros((EXT, LANES), jnp.float32)
        for slot in range(8):
            index = 8 * group + slot
            if index >= COMPS * PAIRS + 2:
                continue
            for half, value in enumerate(pair(index)):
                at = 64 * half + 8 * slot
                here = (lanes >= at) & (lanes < at + 8)
                west = jnp.where(here, turned(at)(value), west)
                east = jnp.where(here, turned(at + HALO)(value), east)
        west_ref[group] = west
        east_ref[group] = east


def steps_kernel(
    lat_ref, fields_ref, bottom_ref, coriolis_ref, first_ref, second_ref, from_west_ref, from_east_ref,
    out_ref, raw, ping, pong, wet, count, lap, flat,
):
    even = lat_ref[0] % 2 == 0
    lanes = lane_ids(EXT)
    upper = lanes >= 64
    place = lanes % 64

    def at(comp, slab):
        return (comp * SLABS + slab) * PITCH + 8

    def put(ref, start, value):
        ref[pl.ds(start, value.shape[0]), :] = value

    def ext(plane, own):
        return jnp.concatenate(extended(plane, own, first_ref, second_ref, even), axis=0)

    def strip(index, low, high):
        group, slot = divmod(index, 8)
        value = jnp.where(upper, turned(64 + 8)(high), turned(8)(low))
        value = jnp.where((place >= 24) & (place < 40), jnp.where(upper, turned(64 + 40)(high), turned(40)(low)), value)
        value = jnp.where(place < 8, turned(-8 * slot)(from_west_ref[group]), value)
        value = jnp.where((place >= 40) & (place < 48), turned(40 - 8 * slot)(from_east_ref[group]), value)
        return value

    bottom = ext(PLANES - 2, bottom_ref[...].astype(jnp.float32))
    bottom_strip = strip(COMPS * PAIRS, bottom, bottom)
    twist = ext(PLANES - 1, coriolis_ref[...])
    twist_strip = strip(COMPS * PAIRS + 1, twist, twist)
    for slot, value in enumerate((bottom, bottom_strip, STEP_DT * twist, STEP_DT * twist_strip)):
        put(flat, slot * PITCH + 8, value)
    high_level = jnp.where(upper, float(PAIRS), 0.0)
    for slab in range(SLABS):
        if slab < LEVELS:
            value = jnp.where(bottom > slab, 1.0, 0.0)
        else:
            value = jnp.where(bottom_strip > (slab - LEVELS) + high_level, 1.0, 0.0)
        put(wet, slab * PITCH + 8, value)
    for slab in range(SLABS):
        start = slab * PITCH + 8
        value = wet[pl.ds(start, EXT), :]
        around = (wet[pl.ds(start - 1, EXT), :] + wet[pl.ds(start + 1, EXT), :]) + beside(value)
        put(count, start, around)

    for comp in range(COMPS):
        for level in range(PAIRS):
            low = ext(comp * LEVELS + level, fields_ref[comp, level])
            high = ext(comp * LEVELS + level + PAIRS, fields_ref[comp, level + PAIRS])
            both = strip(comp * PAIRS + level, low, high)
            for slab, value in ((level, low), (level + PAIRS, high), (LEVELS + level, both)):
                put(raw, at(comp, slab), value)
                put(ping, at(comp, slab), value * wet[pl.ds(slab * PITCH + 8, EXT), :])

    def advance(step, slabs, source, target, a_window, b_window, finish=None):
        a_row, a_rows = a_window
        b_row, b_rows = b_window
        aligned = a_window == b_window
        is_strip = slabs[0] >= LEVELS
        slope_of = raw if step == 0 else source
        bottom_at = (1 if is_strip else 0) * PITCH + 8
        twist_at = (3 if is_strip else 2) * PITCH + 8
        b_lanes = lane_ids(b_rows)

        def body(slab, carry):
            press_east, press_north = carry
            mask_at = pl.multiple_of(slab * PITCH, 8) + 8
            w_a = wet[pl.ds(mask_at + a_row, a_rows), :]
            n_a = count[pl.ds(mask_at + a_row, a_rows), :]
            if aligned:
                w_b, n_b = w_a, n_a
            else:
                w_b = wet[pl.ds(mask_at + b_row, b_rows), :]
                n_b = count[pl.ds(mask_at + b_row, b_rows), :]
            east_slope, centre = [], []
            for comp in range(COMPS):
                start = pl.multiple_of((comp * SLABS + slab) * PITCH, 8) + 8
                value = source[pl.ds(start + a_row, a_rows), :]
                north = source[pl.ds(start + a_row + 1, a_rows), :]
                south = source[pl.ds(start + a_row - 1, a_rows), :]
                if step > 0 and aligned:
                    lateral, slope = beside_and_sloped(value)
                else:
                    lateral = beside(value)
                put(lap, comp * PITCH + 8 + a_row, w_a * ((north + south) + lateral - n_a * value))
                if step == 0:
                    slope = sloped(raw[pl.ds(start + b_row, b_rows), :])
                elif not aligned:
                    value = source[pl.ds(start + b_row, b_rows), :]
                    slope = sloped(value)
                east_slope.append(slope)
                centre.append(value)
            north_slope = []
            for comp in range(COMPS):
                start = pl.multiple_of((comp * SLABS + slab) * PITCH, 8) + 8
                north_slope.append(slope_of[pl.ds(start + b_row + 2, b_rows), :] - slope_of[pl.ds(start + b_row - 2, b_rows), :])
            scale = 0.5 * STEP_DT * GRAVITY
            press_east = press_east + (scale * BETA_S) * east_slope[1] - (scale * ALPHA_T) * east_slope[0]
            press_north = press_north + (scale * BETA_S) * north_slope[1] - (scale * ALPHA_T) * north_slope[0]
            twist_b = flat[pl.ds(twist_at + b_row, b_rows), :]
            bottom_b = flat[pl.ds(bottom_at + b_row, b_rows), :]
            if is_strip:
                level = (slab - LEVELS).astype(jnp.float32) + jnp.where(b_lanes >= 64, float(PAIRS), 0.0)
            else:
                level = slab.astype(jnp.float32)
            keep = 1.0 - jnp.where(bottom_b - 1.0 == level, STEP_DT * DRAG_RATE, 0.0)
            zonal = (-0.5 * STEP_DT) * centre[2]
            merid = (-0.5 * STEP_DT) * centre[3]
            for comp in range(COMPS):
                start = pl.multiple_of((comp * SLABS + slab) * PITCH, 8) + 8
                lap_at = comp * PITCH + 8 + b_row
                value = lap[pl.ds(lap_at, b_rows), :]
                around = lap[pl.ds(lap_at + 1, b_rows), :] + lap[pl.ds(lap_at - 1, b_rows), :]
                smooth = around + beside(value) - n_b * value
                new = zonal * east_slope[comp] + merid * north_slope[comp] - (STEP_DT * KAPPA) * smooth
                if comp < 2:
                    new = new + centre[comp]
                elif comp == 2:
                    new = new + (keep * centre[2] + twist_b * centre[3] - press_east)
                else:
                    new = new + (keep * centre[3] - twist_b * centre[2] - press_north)
                new = w_b * new
                if finish is None:
                    put(target, start + b_row, new)
                else:
                    finish(comp, slab, new)
            return press_east, press_north

        if is_strip:
            total = None
            for slab in slabs:
                salt = slope_of[pl.ds(at(1, slab), EXT), :]
                heat = slope_of[pl.ds(at(0, slab), EXT), :]
                term = BETA_S * salt - ALPHA_T * heat
                total = term if total is None else total + term
            base = (0.5 * STEP_DT * GRAVITY) * jnp.where(upper, turned(64)(total), 0.0)
            base_at = 4 * PITCH + 8
            put(flat, base_at, base)
            middle = flat[pl.ds(base_at + b_row, b_rows), :]
            carry = (
                sloped(middle),
                flat[pl.ds(base_at + b_row + 2, b_rows), :] - flat[pl.ds(base_at + b_row - 2, b_rows), :],
            )
        else:
            carry = (jnp.zeros((b_rows, LANES), jnp.float32),) * 2
        lax.fori_loop(slabs[0], slabs[-1] + 1, body, carry)

    own_lanes = lane_ids(ROWS)

    def finish(comp, slab, new):
        high = slab >= PAIRS
        start = pl.multiple_of((comp * SLABS + LEVELS + slab % PAIRS) * PITCH, 8) + 8 + HALO
        edge = ping[pl.ds(start, ROWS), :]
        edge = jnp.where(high, turned(64)(edge), edge)
        new = jnp.where(own_lanes < 8, turned(-8)(edge), new)
        new = jnp.where(own_lanes >= 120, turned(120 - 32)(edge), new)
        out_ref[comp, slab] = new

    windows = (
        ((0, EXT), (0, EXT)),
        ((0, EXT), (0, EXT)),
        ((4, EXT - 8), (4, EXT - 8)),
        ((4, EXT - 8), (HALO, ROWS)),
    )
    for slabs in (range(LEVELS, SLABS), range(LEVELS)):
        source, target = ping, pong
        for step in range(STEPS):
            last = step == STEPS - 1 and slabs[0] == 0
            advance(step, slabs, source, target, *windows[step], finish if last else None)
            source, target = target, source


def vmem(count):
    return [pl.BlockSpec(memory_space=pltpu.VMEM)] * count


def call(kernel, out_shape, scratch, flops, moved, *operands):
    lat, *arrays = operands
    return pl.pallas_call(
        kernel,
        out_shape=out_shape,
        in_specs=[pl.BlockSpec(memory_space=pltpu.SMEM)] + vmem(len(arrays)),
        out_specs=jax.tree.map(lambda _: pl.BlockSpec(memory_space=pltpu.VMEM), out_shape),
        scratch_shapes=scratch,
        compiler_params=pltpu.CompilerParams(vmem_limit_bytes=32 << 20),
        cost_estimate=pl.CostEstimate(flops=flops, bytes_accessed=moved, transcendentals=0),
    )(lat, *arrays)


def local(fields, sea_mask, bottom_level, coriolis):
    del sea_mask
    lat_count, lon_count = lax.axis_size("lat"), lax.axis_size("lon")
    lat = lax.axis_index("lat").astype(jnp.int32).reshape(1)
    axes = ("lon", "lat")
    flat = lambda lon, row: (lon % lon_count) * lat_count + row
    f32 = lambda *shape: jax.ShapeDtypeStruct(shape, jnp.float32)

    everywhere = [(lon, row) for lon in range(lon_count) for row in range(lat_count)]
    first_pairs = [(flat(lon, row), flat(lon, row ^ 1)) for lon, row in everywhere]
    second_pairs = []
    for lon, row in everywhere:
        if row == lat_count - 1:
            second_pairs.append((flat(lon, row), flat(lon_count - 1 - lon, row)))
        elif row > 0:
            second_pairs.append((flat(lon, row), flat(lon, ((row + 1) ^ 1) - 1)))
    east_pairs = [(flat(lon, row), flat(lon + 1, row)) for lon, row in everywhere]
    west_pairs = [(flat(lon, row), flat(lon - 1, row)) for lon, row in everywhere]

    lat_message = f32(PLANES, HALO, LANES)
    to_first, to_second = call(
        functools.partial(pack_lat_kernel, lat_count=lat_count), (lat_message,) * 2, (), 10**5, 10**6,
        lat, fields, bottom_level, coriolis,
    )
    second = lax.ppermute(to_second, axes, second_pairs)
    first = lax.ppermute(to_first, axes, first_pairs)
    lon_message = f32(GROUPS, EXT, LANES)
    to_west, to_east = call(
        pack_lon_kernel, (lon_message,) * 2, (), 10**5, 10**6,
        lat, fields, bottom_level, coriolis, first, second,
    )
    from_west = lax.ppermute(to_east, axes, east_pairs)
    from_east = lax.ppermute(to_west, axes, west_pairs)
    state = pltpu.VMEM((COMPS * SLABS * PITCH, LANES), jnp.float32)
    masks = pltpu.VMEM((SLABS * PITCH, LANES), jnp.float32)
    scratch = (state, state, state, masks, masks) + (
        pltpu.VMEM((COMPS * PITCH, LANES), jnp.float32), pltpu.VMEM((5 * PITCH, LANES), jnp.float32),
    )
    return call(
        steps_kernel, f32(COMPS, LEVELS, ROWS, LANES), scratch, 2 * 10**7, 10**6,
        lat, fields, bottom_level, coriolis, first, second, from_west, from_east,
    )


def solution(mesh):
    in_specs = (P(None, None, "lat", "lon"), P(None, "lat", "lon"), P("lat", "lon"), P("lat", "lon"))
    out_specs = P(None, None, "lat", "lon")
    return jax.shard_map(local, mesh=mesh, in_specs=in_specs, out_specs=out_specs, check_vma=False)
```

time: 341 us -> 57.2 us (0.17)
  the two profiles are of different devices: /device:TPU:24 before, /device:TPU:27 now
where the time goes in v1:
time: 57.2 us; the launch traced here: 57 us
  starting transfers between devices  24.1 us (42%)
  Pallas kernels  21 us (37%)
  waiting for transfers between devices  9.45 us (17%)
  local copies, waits for them, and re-layouts  2.36 us (4%)
    pallas_call x3, Pallas kernels, call(): pl.pallas_call(kernel, out_shape=out_shape, in_specs=[pl.BlockSpec(memory...  21 us
    ppermute x1, starting transfers between devices, local(): second = lax.ppermute(to_second, axes, second_pairs)  12.7 us
    ppermute x1, waiting for transfers between devices, local(): second = lax.ppermute(to_second, axes, second_pairs)  8.3 us
    ppermute x1, starting transfers between devices, local(): from_east = lax.ppermute(to_west, axes, west_pairs)  6.98 us
    ppermute x1, starting transfers between devices, local(): first = lax.ppermute(to_first, axes, first_pairs)  2.47 us
    unnamed x6, local copies, waits for them, and re-layouts  2.36 us
    ppermute x1, starting transfers between devices, local(): from_west = lax.ppermute(to_east, axes, east_pairs)  1.92 us
    ppermute x1, waiting for transfers between devices, local(): from_east = lax.ppermute(to_west, axes, west_pairs)  1.15 us
  transfers between devices with their start and end apart: 4, of which 2 were waited for; matrix products, arithmetic and copies ran while one was open for 0% of the time, Pallas kernels for 0%

profile of v1, /device:TPU:27, one launch (start us, length us, event | category | flops | bytes accessed | tf_op | source)
XLA Modules:
  0.0 57.0 jit_solution(6956120051923788804)
XLA Ops:
  0.0 0.0 copy-start
  0.0 1.0 %copy-done = f32[4,10,16,128]{3,2,1,0:T(8,128)S(1)} copy-done((f32[4,10,16,128]{3,2,1,0:T(8,128)S(1)}, f32[4,10,16,128]{3,2,1,0:T(8,128)}, u32[]{:S(2)}) %copy-start) | copy-done | bytes 327704
  1.0 0.0 copy-start.1
  1.0 0.7 %copy-done.1 = s32[16,128]{1,0:T(8,128)S(1)} copy-done((s32[16,128]{1,0:T(8,128)S(1)}, s32[16,128]{1,0:T(8,128)}, u32[]{:S(2)}) %copy-start.1) | copy-done | bytes 8216
  1.7 0.0 copy-start.2
  1.7 0.7 %copy-done.2 = f32[16,128]{1,0:T(8,128)S(1)} copy-done((f32[16,128]{1,0:T(8,128)S(1)}, f32[16,128]{1,0:T(8,128)}, u32[]{:S(2)}) %copy-start.2) | copy-done | bytes 8216
  2.4 0.1 shard_map.37
  2.5 2.5 %collective-permute-start = (f32[42,8,128]{2,1,0:T(8,128)S(1)}, f32[42,8,128]{2,1,0:T(8,128)S(1)}, u32[]{:S(2)}, u32[]{:S(2)}) collective-permute-start(f32[42,8,128]{2,1,0:T(8,128)S(1)} %get-tuple-element.9), channel_id=1, source_target_pairs={{0,1},{1,0},{2,3},{3,2},{4,5},{5,4},{6,7},{7,6},{8,9},{9,8},{10,11... | collective-permute-start | bytes 516104 | tf_op jit(solution)/shard_map/ppermute | solution.py:340
  5.0 12.7 %collective-permute-start.1 = (f32[42,8,128]{2,1,0:T(8,128)S(1)}, f32[42,8,128]{2,1,0:T(8,128)S(1)}, u32[]{:S(2)}, u32[]{:S(2)}) collective-permute-start(f32[42,8,128]{2,1,0:T(8,128)S(1)} %get-tuple-element.10), channel_id=1, source_target_pairs={{1,2},{2,1},{3,4},{4,3},{5,6},{6,5},{7,8},{8,7},{9,10},{10,9},{11,... | collective-permute-start | bytes 516104 | tf_op jit(solution)/shard_map/ppermute | solution.py:339
  17.7 0.0 collective-permute-done.first_ref
  17.7 8.3 %collective-permute-done.1.second_ref = f32[42,8,128]{2,1,0:T(8,128)S(1)} collective-permute-done((f32[42,8,128]{2,1,0:T(8,128)S(1)}, f32[42,8,128]{2,1,0:T(8,128)S(1)}, u32[]{:S(2)}, u32[]{:S(2)}) %collective-permute-start.1) | collective-permute-done | bytes 172064 | tf_op jit(solution)/shard_map/ppermute | solution.py:339
  26.0 0.4 shard_map.38
  26.4 1.9 %collective-permute-start.2 = (f32[3,32,128]{2,1,0:T(8,128)S(1)}, f32[3,32,128]{2,1,0:T(8,128)S(1)}, u32[]{:S(2)}, u32[]{:S(2)}) collective-permute-start(f32[3,32,128]{2,1,0:T(8,128)S(1)} %get-tuple-element.11), channel_id=1, source_target_pairs={{0,16},{1,17},{2,18},{3,19},{4,20},{5,21},{6,22},{7,23},{8,24},{9,... | collective-permute-start | bytes 147464 | tf_op jit(solution)/shard_map/ppermute | solution.py:346
  28.3 7.0 %collective-permute-start.3 = (f32[3,32,128]{2,1,0:T(8,128)S(1)}, f32[3,32,128]{2,1,0:T(8,128)S(1)}, u32[]{:S(2)}, u32[]{:S(2)}) collective-permute-start(f32[3,32,128]{2,1,0:T(8,128)S(1)} %get-tuple-element.12), channel_id=1, source_target_pairs={{0,496},{1,497},{2,498},{3,499},{4,500},{5,501},{6,502},{7,503},{8... | collective-permute-start | bytes 147464 | tf_op jit(solution)/shard_map/ppermute | solution.py:347
  35.3 0.0 collective-permute-done.2.from_west_ref
  35.3 1.1 %collective-permute-done.3.from_east_ref = f32[3,32,128]{2,1,0:T(8,128)S(1)} collective-permute-done((f32[3,32,128]{2,1,0:T(8,128)S(1)}, f32[3,32,128]{2,1,0:T(8,128)S(1)}, u32[]{:S(2)}, u32[]{:S(2)}) %collective-permute-start.3) | collective-permute-done | bytes 49184 | tf_op jit(solution)/shard_map/ppermute | solution.py:347
  36.5 20.5 %shard_map.39 = f32[4,10,16,128]{3,2,1,0:T(8,128)} custom-call(s32[1]{0:T(128)} %bitcast.lat_ref, f32[4,10,16,128]{3,2,1,0:T(8,128)S(1)} %copy-done, s32[16,128]{1,0:T(8,128)S(1)} %copy-done.1, f32[16,128]{1,0:T(8,128)S(1)} %copy-done.2, f32[42,8,128]{2,1,0:T(8,128)S(1)} %collective-permute-done.first_ref, ...), custom_call_target="tpu_custom_call" | custom-call | flops 20000000 | bytes 1000000 | tf_op jit(solution)/shard_map/pallas_call | solution.py:304
Async XLA Ops:
  0.0 1.0 %copy-start = (f32[4,10,16,128]{3,2,1,0:T(8,128)S(1)}, f32[4,10,16,128]{3,2,1,0:T(8,128)}, u32[]{:S(2)}) copy-start(f32[4,10,16,128]{3,2,1,0:T(8,128)} %fields_ref.5) | copy-start | bytes 983044
  1.0 0.7 %copy-start.1 = (s32[16,128]{1,0:T(8,128)S(1)}, s32[16,128]{1,0:T(8,128)}, u32[]{:S(2)}) copy-start(s32[16,128]{1,0:T(8,128)} %bottom_ref.5) | copy-start | bytes 24580
  1.7 0.7 %copy-start.2 = (f32[16,128]{1,0:T(8,128)S(1)}, f32[16,128]{1,0:T(8,128)}, u32[]{:S(2)}) copy-start(f32[16,128]{1,0:T(8,128)} %coriolis_ref.5) | copy-start | bytes 24580
  2.5 15.2 %collective-permute-start = (f32[42,8,128]{2,1,0:T(8,128)S(1)}, f32[42,8,128]{2,1,0:T(8,128)S(1)}, u32[]{:S(2)}, u32[]{:S(2)}) collective-permute-start(f32[42,8,128]{2,1,0:T(8,128)S(1)} %get-tuple-element.9), channel_id=1, source_target_pairs={{0,1},{1,0},{2,3},{3,2},{4,5},{5,4},{6,7},{7,6},{8,9},{9,8},{10,11... | collective-permute-start | bytes 516104 | tf_op jit(solution)/shard_map/ppermute | solution.py:340
  5.0 21.0 %collective-permute-start.1 = (f32[42,8,128]{2,1,0:T(8,128)S(1)}, f32[42,8,128]{2,1,0:T(8,128)S(1)}, u32[]{:S(2)}, u32[]{:S(2)}) collective-permute-start(f32[42,8,128]{2,1,0:T(8,128)S(1)} %get-tuple-element.10), channel_id=1, source_target_pairs={{1,2},{2,1},{3,4},{4,3},{5,6},{6,5},{7,8},{8,7},{9,10},{10,9},{11,... | collective-permute-start | bytes 516104 | tf_op jit(solution)/shard_map/ppermute | solution.py:339
  26.4 8.9 %collective-permute-start.2 = (f32[3,32,128]{2,1,0:T(8,128)S(1)}, f32[3,32,128]{2,1,0:T(8,128)S(1)}, u32[]{:S(2)}, u32[]{:S(2)}) collective-permute-start(f32[3,32,128]{2,1,0:T(8,128)S(1)} %get-tuple-element.11), channel_id=1, source_target_pairs={{0,16},{1,17},{2,18},{3,19},{4,20},{5,21},{6,22},{7,23},{8,24},{9,... | collective-permute-start | bytes 147464 | tf_op jit(solution)/shard_map/ppermute | solution.py:346
  28.3 8.1 %collective-permute-start.3 = (f32[3,32,128]{2,1,0:T(8,128)S(1)}, f32[3,32,128]{2,1,0:T(8,128)S(1)}, u32[]{:S(2)}, u32[]{:S(2)}) collective-permute-start(f32[3,32,128]{2,1,0:T(8,128)S(1)} %get-tuple-element.12), channel_id=1, source_target_pairs={{0,496},{1,497},{2,498},{3,499},{4,500},{5,501},{6,502},{7,503},{8... | collective-permute-start | bytes 147464 | tf_op jit(solution)/shard_map/ppermute | solution.py:347

commit v2 on v0

v2 whole, which is shorter than its diff:
```python
import functools

import jax
import jax.numpy as jnp
from jax import lax
from jax.experimental import pallas as pl
from jax.experimental.pallas import tpu as pltpu
from jax.sharding import PartitionSpec as P

STEPS = 4
STEP_DT = 0.1
KAPPA = 0.2
DRAG_RATE = 0.5
GRAVITY = 0.1
ALPHA_T = 0.2
BETA_S = 0.15

COMPS = 4
LEVELS = 10
PAIRS = LEVELS // 2
PLANES = COMPS * LEVELS + 2
ROWS = 16
HALO = 8
EXT = ROWS + 2 * HALO
PITCH = EXT + 16
LANES = 128
BATCH = 5
LAG = 1
LIMIT = 56
GROUPS = 3


def lane_ids(rows):
    return lax.broadcasted_iota(jnp.int32, (rows, LANES), 1)


def turned(by):
    if by % LANES == 0:
        return lambda value: value
    return lambda value: pltpu.roll(value, by % LANES, 1)


def beside(value):
    return turned(-1)(value) + turned(1)(value)


def sloped(value):
    return turned(-2)(value) - turned(2)(value)


def in_two(value):
    high = value.astype(jnp.bfloat16)
    low = (value - high.astype(jnp.float32)).astype(jnp.bfloat16)
    return jnp.concatenate([high, low], axis=1)


def neighbours():
    source = lax.broadcasted_iota(jnp.int32, (2 * LANES, 2 * LANES), 0) % LANES
    target = lax.broadcasted_iota(jnp.int32, (2 * LANES, 2 * LANES), 1)
    east = (source - target) % LANES
    sums = jnp.where((east == 1) | (east == LANES - 1), 1.0, 0.0)
    slopes = jnp.where(east == 2, 1.0, jnp.where(east == LANES - 2, -1.0, 0.0))
    return jnp.where(target < LANES, sums, slopes).astype(jnp.bfloat16)


def pairs_of(plane_of):
    for index in range(COMPS * PAIRS + 2):
        comp, level = divmod(index, PAIRS)
        if comp < COMPS:
            low = plane_of(comp * LEVELS + level)
            yield index, low, plane_of(comp * LEVELS + level + PAIRS)
        else:
            value = plane_of(COMPS * LEVELS + index - COMPS * PAIRS)
            yield index, value, value


def plane_reader(fields_ref, flat_ref):
    def read(plane, start, rows):
        if plane >= COMPS * LEVELS:
            return flat_ref[plane - COMPS * LEVELS, pl.ds(start, rows), :]
        return fields_ref[plane // LEVELS, plane % LEVELS, pl.ds(start, rows), :]

    return read


def folded(value, lanes):
    rows = HALO - 1 - lax.broadcasted_iota(jnp.int32, (HALO, LANES), 0)
    return jnp.take_along_axis(jnp.take_along_axis(value, lanes, axis=1), rows, axis=0)


def pack_second_kernel(
    lat_ref, fields_any, bottom_any, coriolis_any, second_ref, rows_ref, bottom_ref, coriolis_ref, semaphores, *, lat_count
):
    lat = lat_ref[0]
    row = pl.multiple_of(jnp.where(lat % 2 == 0, 0, HALO), HALO)
    here = pl.ds(row, HALO)
    copies = [
        pltpu.make_async_copy(source, target, semaphores.at[index])
        for index, (source, target) in enumerate((
            (fields_any.at[:, :, here, :], rows_ref),
            (bottom_any.at[here, :], bottom_ref),
            (coriolis_any.at[here, :], coriolis_ref),
        ))
    ]
    for copy in copies:
        copy.start()
    for copy in copies:
        copy.wait()

    def read(plane):
        if plane < COMPS * LEVELS:
            return rows_ref[plane // LEVELS, plane % LEVELS]
        return bottom_ref[...].astype(jnp.float32) if plane == PLANES - 2 else coriolis_ref[...]

    second_ref[PLANES] = jnp.zeros((HALO, LANES), jnp.float32)

    @pl.when(lat < lat_count - 1)
    def _():
        for plane in range(PLANES):
            second_ref[plane] = read(plane)

    @pl.when(lat == lat_count - 1)
    def _():
        back = LANES - 1 - lane_ids(HALO)
        for plane in range(PLANES):
            value = folded(read(plane), back)
            second_ref[plane] = -value if 2 * LEVELS <= plane < 4 * LEVELS else value


def pack_first_kernel(lat_ref, fields_ref, flat_ref, first_ref):
    read = plane_reader(fields_ref, flat_ref)
    row = pl.multiple_of(jnp.where(lat_ref[0] % 2 == 0, HALO, 0), HALO)
    for plane in range(PLANES):
        first_ref[plane] = read(plane, row, HALO)


def pack_sides_kernel(lat_ref, lon_ref, fields_ref, flat_ref, second_ref, first_ref, to_second_ref, to_first_ref):
    read, joined = plane_reader(fields_ref, flat_ref), joiner(lat_ref)
    lanes = lane_ids(EXT)
    west = [jnp.zeros((EXT, LANES), jnp.float32) for _ in range(GROUPS)]
    east = list(west)
    for index, low, high in pairs_of(lambda plane: joined(first_ref[plane], read(plane, 0, ROWS), second_ref[plane])):
        group, slot = divmod(index, 8)
        for at, value in ((8 * slot, low), (8 * slot + 64, high)):
            here = (lanes >= at) & (lanes < at + 8)
            west[group] = jnp.where(here, turned(at)(value), west[group])
            east[group] = jnp.where(here, turned(at + HALO)(value), east[group])
    for group in range(GROUPS):
        even = lon_ref[0] % 2 == 0
        to_second_ref[group] = jnp.where(even, west[group], east[group])
        to_first_ref[group] = jnp.where(even, east[group], west[group])


def joiner(lat_ref):
    even = lat_ref[0] % 2 == 0

    def joined(one, own, two):
        return jnp.concatenate([jnp.where(even, two, one), own, jnp.where(even, one, two)], axis=0)

    return joined


def evolve(scratch, slabs, strips, plain_of, bottom, twist, finish):
    raw, state, lap, east_diff, north_diff, wet, count, flat, press, matrix = scratch

    def at(slab, comp=0):
        return (comp * slabs + slab) * PITCH + 8

    def get(ref, start, rows):
        return ref[pl.ds(start, rows), :]

    def put(ref, start, value):
        ref[pl.ds(start, value.shape[0]), :] = value

    matrix[...] = neighbours()
    if strips:
        bottom = bottom - jnp.where(lane_ids(EXT) >= 64, float(PAIRS), 0.0)
    put(flat, 8, bottom)
    put(flat, PITCH + 8, STEP_DT * twist)
    for slab in range(slabs):
        value = jnp.where(bottom > float(slab), 1.0, 0.0)
        put(wet, at(slab), value)
        around = (get(wet, at(slab) - 1, EXT) + get(wet, at(slab) + 1, EXT)) + beside(value)
        put(count, at(slab), around)
        for comp in range(COMPS):
            plain = plain_of(comp, slab)
            put(raw, at(slab, comp), plain)
            put(state, at(slab, comp), plain * value)

    a_windows = ((0, EXT), (0, EXT), (4, EXT - 8), (0, EXT))
    b_windows = ((0, EXT), (0, EXT), (4, EXT - 8), (HALO, ROWS))

    def before(step, batch):
        a_row, a_rows = a_windows[step]
        b_row, b_rows = b_windows[step]
        slope_of = raw if step == 0 else state
        fields = [(slab, comp) for slab in batch for comp in range(COMPS)]

        def lateral(ref):
            values = [in_two(get(ref, at(*field) + a_row, a_rows)) for field in fields]
            return jnp.dot(jnp.concatenate(values, axis=0), matrix[...], preferred_element_type=jnp.float32)

        both = lateral(state)
        slopes = lateral(raw) if step == 0 else both
        for index, (slab, comp) in enumerate(fields):
            w = get(wet, at(slab) + a_row, a_rows)
            n = get(count, at(slab) + a_row, a_rows)
            start = at(slab, comp)
            value = get(state, start + a_row, a_rows)
            along = get(state, start + a_row + 1, a_rows) + get(state, start + a_row - 1, a_rows)
            sums = both[index * a_rows : (index + 1) * a_rows, :LANES]
            put(lap, start + a_row, w * (along + sums - n * value))
            first = index * a_rows + b_row - a_row
            put(east_diff, start + b_row, slopes[first : first + b_rows, LANES:])
            put(north_diff, start + b_row, get(slope_of, start + b_row + 2, b_rows) - get(slope_of, start + b_row - 2, b_rows))

    scale = 0.5 * STEP_DT * GRAVITY

    def heavier(ref, slab, row, rows):
        return (scale * BETA_S) * get(ref, at(slab, 1) + row, rows) - (scale * ALPHA_T) * get(ref, at(slab, 0) + row, rows)

    def base(step):
        row, rows = b_windows[step]
        for slot, ref in enumerate((east_diff, north_diff)):
            total = None
            for slab in range(slabs):
                term = heavier(ref, slab, row, rows)
                total = term if total is None else total + term
            put(press, slot * PITCH + 8 + row, jnp.where(lane_ids(rows) >= 64, turned(64)(total), 0.0))

    def after(step, slab):
        row, rows = b_windows[step]
        w = get(wet, at(slab) + row, rows)
        n = get(count, at(slab) + row, rows)
        slopes = []
        for slot, ref in enumerate((east_diff, north_diff)):
            slope = heavier(ref, slab, row, rows)
            press_at = slot * PITCH + 8 + row
            if slab > 0 or strips:
                slope = slope + get(press, press_at, rows)
            put(press, press_at, slope)
            slopes.append(slope)
        twist_b = get(flat, PITCH + 8 + row, rows)
        bottom_b = get(flat, 8 + row, rows)
        keep = jnp.where(bottom_b == float(slab + 1), 1.0 - STEP_DT * DRAG_RATE, 1.0)
        old_zonal = get(state, at(slab, 2) + row, rows)
        old_merid = get(state, at(slab, 3) + row, rows)
        zonal = (-0.5 * STEP_DT) * old_zonal
        merid = (-0.5 * STEP_DT) * old_merid
        for comp in range(COMPS):
            start = at(slab, comp) + row
            value = get(lap, start, rows)
            along = get(lap, start + 1, rows) + get(lap, start - 1, rows)
            smooth = along + beside(value) - n * value
            new = zonal * get(east_diff, start, rows) + merid * get(north_diff, start, rows) - (STEP_DT * KAPPA) * smooth
            if comp < 2:
                new = new + get(state, start, rows)
            elif comp == 2:
                new = new + (keep * old_zonal + twist_b * old_merid - slopes[0])
            else:
                new = new + (keep * old_merid - twist_b * old_zonal - slopes[1])
            new = w * new
            if step < STEPS - 1:
                put(state, start, new)
            else:
                finish(comp, slab, new)

    batches = [tuple(range(first, min(first + BATCH, slabs))) for first in range(0, slabs, BATCH)]
    for batch in batches:
        before(0, batch)
    for step in range(STEPS):
        if strips:
            base(step)
        waiting = []
        for batch in batches:
            for slab in batch:
                after(step, slab)
            waiting.append(batch)
            if step < STEPS - 1 and len(waiting) > LAG:
                before(step + 1, waiting.pop(0))
        if step < STEPS - 1:
            for batch in waiting:
                before(step + 1, batch)


def block_kernel(lat_ref, fields_ref, flat_ref, second_ref, first_ref, out_ref, *scratch):
    read, joined = plane_reader(fields_ref, flat_ref), joiner(lat_ref)

    def ext(plane):
        return joined(first_ref[plane], read(plane, 0, ROWS), second_ref[plane])

    def finish(comp, slab, new):
        out_ref[comp, slab] = new

    evolve(
        scratch, LEVELS, False, lambda comp, slab: ext(comp * LEVELS + slab), ext(PLANES - 2), ext(PLANES - 1), finish
    )


def strips_kernel(
    lat_ref, lon_ref, fields_ref, flat_ref, second_ref, first_ref, second_side_ref, first_side_ref, block_ref, out_ref, *scratch
):
    read, joined = plane_reader(fields_ref, flat_ref), joiner(lat_ref)
    lanes = lane_ids(EXT)
    upper = lanes >= 64
    place = lanes % 64

    def ext(plane):
        return joined(first_ref[plane], read(plane, 0, ROWS), second_ref[plane])

    even = lon_ref[0] % 2 == 0
    from_west = [jnp.where(even, second_side_ref[group], first_side_ref[group]) for group in range(GROUPS)]
    from_east = [jnp.where(even, first_side_ref[group], second_side_ref[group]) for group in range(GROUPS)]

    def strip(index, low, high):
        group, slot = divmod(index, 8)
        value = jnp.where(upper, turned(64 + 8)(high), turned(8)(low))
        value = jnp.where((place >= 24) & (place < 40), jnp.where(upper, turned(64 + 40)(high), turned(40)(low)), value)
        value = jnp.where(place < 8, turned(-8 * slot)(from_west[group]), value)
        value = jnp.where((place >= 40) & (place < 48), turned(40 - 8 * slot)(from_east[group]), value)
        return value

    def plain_of(comp, slab):
        return strip(comp * PAIRS + slab, ext(comp * LEVELS + slab), ext(comp * LEVELS + slab + PAIRS))

    bottom, twist = ext(PLANES - 2), ext(PLANES - 1)
    own_lanes = lane_ids(ROWS)

    def finish(comp, slab, new):
        for half in range(2):
            level = slab + half * PAIRS
            value = block_ref[comp, level]
            value = jnp.where(own_lanes < 8, turned(-8 - 64 * half)(new), value)
            out_ref[comp, level] = jnp.where(own_lanes >= 120, turned(120 - 32 - 64 * half)(new), value)

    evolve(
        scratch, PAIRS, True, plain_of, strip(COMPS * PAIRS, bottom, bottom), strip(COMPS * PAIRS + 1, twist, twist), finish
    )


def call(kernel, out_shape, scratch, flops, moved, *operands, whole=False):
    far = pltpu.HBM if whole else pltpu.VMEM
    places = [pltpu.SMEM if operand.shape == (1,) else far for operand in operands]
    return pl.pallas_call(
        kernel,
        out_shape=out_shape,
        in_specs=[pl.BlockSpec(memory_space=place) for place in places],
        out_specs=jax.tree.map(lambda _: pl.BlockSpec(memory_space=pltpu.VMEM), out_shape),
        scratch_shapes=scratch,
        compiler_params=pltpu.CompilerParams(vmem_limit_bytes=(LIMIT if whole else 24) << 20),
        cost_estimate=pl.CostEstimate(flops=flops, bytes_accessed=moved, transcendentals=0),
    )(*operands)


def scratch_for(slabs):
    rows = lambda planes: pltpu.VMEM((planes * PITCH, LANES), jnp.float32)
    return (rows(COMPS * slabs),) * 5 + (rows(slabs),) * 2 + (rows(2),) * 2 + (pltpu.VMEM((2 * LANES, 2 * LANES), jnp.bfloat16),)


def local(fields, sea_mask, bottom_level, coriolis):
    del sea_mask
    lat_count, lon_count = lax.axis_size("lat"), lax.axis_size("lon")
    lat = lax.axis_index("lat").astype(jnp.int32).reshape(1)
    lon = lax.axis_index("lon").astype(jnp.int32).reshape(1)
    axes = ("lon", "lat")
    index_of = lambda lon, row: (lon % lon_count) * lat_count + row
    f32 = lambda *shape: jax.ShapeDtypeStruct(shape, jnp.float32)

    def other_side(i):
        return ((i + 1) ^ 1) - 1

    everywhere = [(i, j) for i in range(lon_count) for j in range(lat_count)]
    lat_first = [(index_of(i, j), index_of(i, j ^ 1)) for i, j in everywhere]
    lat_second = []
    for i, j in everywhere:
        if j == lat_count - 1:
            lat_second.append((index_of(i, j), index_of(lon_count - 1 - i, j)))
        elif j > 0:
            lat_second.append((index_of(i, j), index_of(i, other_side(j))))
    lon_first = [(index_of(i, j), index_of(i ^ 1, j)) for i, j in everywhere]
    lon_second = [(index_of(i, j), index_of(other_side(i), j)) for i, j in everywhere]

    flat = jnp.stack([bottom_level.astype(jnp.float32), coriolis])
    rows_message, side_message = f32(PLANES, HALO, LANES), f32(GROUPS, EXT, LANES)
    held = (
        pltpu.VMEM((COMPS, LEVELS, HALO, LANES), jnp.float32), pltpu.VMEM((HALO, LANES), jnp.int32),
        pltpu.VMEM((HALO, LANES), jnp.float32), pltpu.SemaphoreType.DMA((3,)),
    )
    to_second = call(
        functools.partial(pack_second_kernel, lat_count=lat_count), f32(PLANES + 1, HALO, LANES), held, 10**5, 10**6,
        lat, fields, bottom_level, coriolis, whole=True,
    )
    second = lax.ppermute(to_second, axes, lat_second)
    to_first = call(pack_first_kernel, rows_message, (), 10**5, 10**6, lat, fields, flat)
    first = lax.ppermute(to_first, axes, lat_first)
    to_second_side, to_first_side = call(
        pack_sides_kernel, (side_message,) * 2, (), 10**5, 10**6, lat, lon, fields, flat, second, first
    )
    second_side = lax.ppermute(to_second_side, axes, lon_second)
    first_side = lax.ppermute(to_first_side, axes, lon_first)
    result = f32(COMPS, LEVELS, ROWS, LANES)
    block = call(block_kernel, result, scratch_for(LEVELS), 10**9, 10**6, lat, fields, flat, second, first)
    return call(
        strips_kernel, result, scratch_for(PAIRS), 10**8, 10**6,
        lat, lon, fields, flat, second, first, second_side, first_side, block,
    )


def solution(mesh):
    in_specs = (P(None, None, "lat", "lon"), P(None, "lat", "lon"), P("lat", "lon"), P("lat", "lon"))
    out_specs = P(None, None, "lat", "lon")
    return jax.shard_map(local, mesh=mesh, in_specs=in_specs, out_specs=out_specs, check_vma=False)
```

time: 341 us -> 39 us (0.11)
  the two profiles are of different devices: /device:TPU:24 before, /device:TPU:27 now
where the time goes in v2:
time: 39 us; the launch traced here: 38.7 us
  starting transfers between devices  23.5 us (60%)
  Pallas kernels  8.41 us (22%)
  waiting for transfers between devices  6.69 us (17%)
    ppermute x1, starting transfers between devices, local(): second = lax.ppermute(to_second, axes, lat_second)  12.7 us
    pallas_call x5, Pallas kernels, call(): pl.pallas_call(kernel, out_shape=out_shape, in_specs=[pl.BlockSpec(memory...  8.41 us
    ppermute x1, starting transfers between devices, local(): second_side = lax.ppermute(to_second_side, axes, lon_second)  6.98 us
    ppermute x1, waiting for transfers between devices, local(): second = lax.ppermute(to_second, axes, lat_second)  5.31 us
    ppermute x1, starting transfers between devices, local(): first = lax.ppermute(to_first, axes, lat_first)  1.92 us
    ppermute x1, starting transfers between devices, local(): first_side = lax.ppermute(to_first_side, axes, lon_first)  1.92 us
    ppermute x1, waiting for transfers between devices, local(): first = lax.ppermute(to_first, axes, lat_first)  1.37 us
  transfers between devices with their start and end apart: 4, of which 2 were waited for; matrix products, arithmetic and copies ran while one was open for 0% of the time, Pallas kernels for 8%

profile of v2, /device:TPU:27, one launch (start us, length us, event | category | flops | bytes accessed | tf_op | source)
XLA Modules:
  0.0 38.7 jit_solution(10522887856359773471)
XLA Ops:
  0.0 0.0 copy-start
  0.0 0.0 copy-start.1
  0.0 1.8 %shard_map.37 = f32[43,8,128]{2,1,0:T(8,128)} custom-call(s32[1]{0:T(128)} %bitcast.lat_ref, f32[4,10,16,128]{3,2,1,0:T(8,128)} %fields_ref.7, s32[16,128]{1,0:T(8,128)} %bottom_any.1, f32[16,128]{1,0:T(8,128)} %coriolis_any.1), custom_call_target="tpu_custom_call" | custom-call | flops 100000 | bytes 1000000 | tf_op jit(solution)/shard_map/pallas_call | solution.py:344
  1.8 0.0 copy-start.2
  1.8 12.7 %collective-permute-start = (f32[43,8,128]{2,1,0:T(8,128)}, f32[43,8,128]{2,1,0:T(8,128)S(1)}, u32[]{:S(2)}, u32[]{:S(2)}) collective-permute-start(f32[43,8,128]{2,1,0:T(8,128)} %shard_map.37), channel_id=1, source_target_pairs={{1,2},{2,1},{3,4},{4,3},{5,6},{6,5},{7,8},{8,7},{9,10},{10,9},{11,... | collective-permute-start | bytes 528392 | tf_op jit(solution)/shard_map/ppermute | solution.py:393
  14.5 0.0 copy-done.1
  14.5 0.0 copy-done.2
  14.6 0.0 copy-done
  14.6 1.9 %collective-permute-start.1 = (f32[42,8,128]{2,1,0:T(8,128)S(1)}, f32[42,8,128]{2,1,0:T(8,128)S(1)}, u32[]{:S(2)}, u32[]{:S(2)}) collective-permute-start(f32[42,8,128]{2,1,0:T(8,128)S(1)} %shard_map.38), channel_id=1, source_target_pairs={{0,1},{1,0},{2,3},{3,2},{4,5},{5,4},{6,7},{7,6},{8,9},{9,8},{10,11... | collective-permute-start | bytes 516104 | tf_op jit(solution)/shard_map/ppermute | solution.py:395
  16.5 1.4 %collective-permute-done.1.first_ref = f32[42,8,128]{2,1,0:T(8,128)S(1)} collective-permute-done((f32[42,8,128]{2,1,0:T(8,128)S(1)}, f32[42,8,128]{2,1,0:T(8,128)S(1)}, u32[]{:S(2)}, u32[]{:S(2)}) %collective-permute-start.1) | collective-permute-done | bytes 172064 | tf_op jit(solution)/shard_map/ppermute | solution.py:395
  17.9 5.3 %collective-permute-done.second_ref = f32[43,8,128]{2,1,0:T(8,128)S(1)} collective-permute-done((f32[43,8,128]{2,1,0:T(8,128)}, f32[43,8,128]{2,1,0:T(8,128)S(1)}, u32[]{:S(2)}, u32[]{:S(2)}) %collective-permute-start) | collective-permute-done | bytes 176160 | tf_op jit(solution)/shard_map/ppermute | solution.py:393
  23.2 0.4 %shard_map.39 = (f32[3,32,128]{2,1,0:T(8,128)S(1)}, f32[3,32,128]{2,1,0:T(8,128)S(1)}) custom-call(s32[1]{0:T(128)} %bitcast.lat_ref, s32[1]{0:T(128)} %bitcast.1.lon_ref, f32[4,10,16,128]{3,2,1,0:T(8,128)S(1)} %copy-done, f32[2,16,128]{2,1,0:T(8,128)S(1)} %pad_maximum_fusion.flat_ref, f32[43,8,128]{2,1,0:T(8,128)S(1)} %collective-permute-done.second_ref, ...), custom_call_target="tpu_custom_call" | custom-call | flops 100000 | bytes 1000000 | tf_op jit(solution)/shard_map/pallas_call | solution.py:344
  23.6 7.0 %collective-permute-start.2 = (f32[3,32,128]{2,1,0:T(8,128)S(1)}, f32[3,32,128]{2,1,0:T(8,128)S(1)}, u32[]{:S(2)}, u32[]{:S(2)}) collective-permute-start(f32[3,32,128]{2,1,0:T(8,128)S(1)} %get-tuple-element.7), channel_id=1, source_target_pairs={{0,496},{1,497},{2,498},{3,499},{4,500},{5,501},{6,502},{7,503},{8... | collective-permute-start | bytes 147464 | tf_op jit(solution)/shard_map/ppermute | solution.py:399
  30.6 1.9 %collective-permute-start.3 = (f32[3,32,128]{2,1,0:T(8,128)S(1)}, f32[3,32,128]{2,1,0:T(8,128)S(1)}, u32[]{:S(2)}, u32[]{:S(2)}) collective-permute-start(f32[3,32,128]{2,1,0:T(8,128)S(1)} %get-tuple-element.8), channel_id=1, source_target_pairs={{0,16},{1,17},{2,18},{3,19},{4,20},{5,21},{6,22},{7,23},{8,24},{9,... | collective-permute-start | bytes 147464 | tf_op jit(solution)/shard_map/ppermute | solution.py:400
  32.6 2.9 %shard_map.40.block_ref = f32[4,10,16,128]{3,2,1,0:T(8,128)S(1)} custom-call(s32[1]{0:T(128)} %bitcast.lat_ref, f32[4,10,16,128]{3,2,1,0:T(8,128)S(1)} %copy-done, f32[2,16,128]{2,1,0:T(8,128)S(1)} %pad_maximum_fusion.flat_ref, f32[43,8,128]{2,1,0:T(8,128)S(1)} %collective-permute-done.second_ref, f32[42,8,128]{2,1,0:T(8,128)S(1)} %collective-permute-done.1.first_ref), custom_call_target="tpu_custom_call" | custom-call | flops 1000000000 | bytes 1000000 | tf_op jit(solution)/shard_map/pallas_call | solution.py:344
  35.5 0.0 collective-permute-done.2.second_side_ref
  35.5 0.0 collective-permute-done.3.first_side_ref
  35.5 3.2 %shard_map.41 = f32[4,10,16,128]{3,2,1,0:T(8,128)} custom-call(s32[1]{0:T(128)} %bitcast.lat_ref, s32[1]{0:T(128)} %bitcast.1.lon_ref, f32[4,10,16,128]{3,2,1,0:T(8,128)S(1)} %copy-done, f32[2,16,128]{2,1,0:T(8,128)S(1)} %pad_maximum_fusion.flat_ref, f32[43,8,128]{2,1,0:T(8,128)S(1)} %collective-permute-done.second_ref, ...), custom_call_target="tpu_custom_call" | custom-call | flops 100000000 | bytes 1000000 | tf_op jit(solution)/shard_map/pallas_call | solution.py:344
  (3 shorter events, 0.0 us)
Async XLA Ops:
  0.0 14.6 %copy-start = (f32[4,10,16,128]{3,2,1,0:T(8,128)S(1)}, f32[4,10,16,128]{3,2,1,0:T(8,128)}, u32[]{:S(2)}) copy-start(f32[4,10,16,128]{3,2,1,0:T(8,128)} %fields_ref.7) | copy-start | bytes 983044
  0.0 14.5 %copy-start.1 = (s32[16,128]{1,0:T(8,128)S(1)}, s32[16,128]{1,0:T(8,128)}, u32[]{:S(2)}) copy-start(s32[16,128]{1,0:T(8,128)} %bottom_any.1) | copy-start | bytes 24580
  1.8 12.7 %copy-start.2 = (f32[16,128]{1,0:T(8,128)S(1)}, f32[16,128]{1,0:T(8,128)}, u32[]{:S(2)}) copy-start(f32[16,128]{1,0:T(8,128)} %coriolis_any.1) | copy-start | bytes 24580
  1.8 21.4 %collective-permute-start = (f32[43,8,128]{2,1,0:T(8,128)}, f32[43,8,128]{2,1,0:T(8,128)S(1)}, u32[]{:S(2)}, u32[]{:S(2)}) collective-permute-start(f32[43,8,128]{2,1,0:T(8,128)} %shard_map.37), channel_id=1, source_target_pairs={{1,2},{2,1},{3,4},{4,3},{5,6},{6,5},{7,8},{8,7},{9,10},{10,9},{11,... | collective-permute-start | bytes 528392 | tf_op jit(solution)/shard_map/ppermute | solution.py:393
  14.6 3.3 %collective-permute-start.1 = (f32[42,8,128]{2,1,0:T(8,128)S(1)}, f32[42,8,128]{2,1,0:T(8,128)S(1)}, u32[]{:S(2)}, u32[]{:S(2)}) collective-permute-start(f32[42,8,128]{2,1,0:T(8,128)S(1)} %shard_map.38), channel_id=1, source_target_pairs={{0,1},{1,0},{2,3},{3,2},{4,5},{5,4},{6,7},{7,6},{8,9},{9,8},{10,11... | collective-permute-start | bytes 516104 | tf_op jit(solution)/shard_map/ppermute | solution.py:395
  23.6 11.8 %collective-permute-start.2 = (f32[3,32,128]{2,1,0:T(8,128)S(1)}, f32[3,32,128]{2,1,0:T(8,128)S(1)}, u32[]{:S(2)}, u32[]{:S(2)}) collective-permute-start(f32[3,32,128]{2,1,0:T(8,128)S(1)} %get-tuple-element.7), channel_id=1, source_target_pairs={{0,496},{1,497},{2,498},{3,499},{4,500},{5,501},{6,502},{7,503},{8... | collective-permute-start | bytes 147464 | tf_op jit(solution)/shard_map/ppermute | solution.py:399
  30.6 4.9 %collective-permute-start.3 = (f32[3,32,128]{2,1,0:T(8,128)S(1)}, f32[3,32,128]{2,1,0:T(8,128)S(1)}, u32[]{:S(2)}, u32[]{:S(2)}) collective-permute-start(f32[3,32,128]{2,1,0:T(8,128)S(1)} %get-tuple-element.8), channel_id=1, source_target_pairs={{0,16},{1,17},{2,18},{3,19},{4,20},{5,21},{6,22},{7,23},{8,24},{9,... | collective-permute-start | bytes 147464 | tf_op jit(solution)/shard_map/ppermute | solution.py:400

commit v3 on v2

--- a/solution.py
+++ b/solution.py
@@ -22,6 +22,8 @@
 ROWS = 16
 HALO = 8
 EXT = ROWS + 2 * HALO
+EARLY = ROWS + HALO
+SPARE = 48
 PITCH = EXT + 16
 LANES = 128
 BATCH = 5
@@ -134,21 +136,46 @@
         first_ref[plane] = read(plane, row, HALO)
 
 
-def pack_sides_kernel(lat_ref, lon_ref, fields_ref, flat_ref, second_ref, first_ref, to_second_ref, to_first_ref):
-    read, joined = plane_reader(fields_ref, flat_ref), joiner(lat_ref)
-    lanes = lane_ids(EXT)
-    west = [jnp.zeros((EXT, LANES), jnp.float32) for _ in range(GROUPS)]
-    east = list(west)
-    for index, low, high in pairs_of(lambda plane: joined(first_ref[plane], read(plane, 0, ROWS), second_ref[plane])):
+def side_tiles(rows, plane_of, shift):
+    lanes = lane_ids(rows)
+    tiles = [jnp.zeros((rows, LANES), jnp.float32) for _ in range(GROUPS)]
+    for index, low, high in pairs_of(plane_of):
         group, slot = divmod(index, 8)
         for at, value in ((8 * slot, low), (8 * slot + 64, high)):
             here = (lanes >= at) & (lanes < at + 8)
-            west[group] = jnp.where(here, turned(at)(value), west[group])
-            east[group] = jnp.where(here, turned(at + HALO)(value), east[group])
+            tiles[group] = jnp.where(here, pltpu.roll(value, at + shift, 1), tiles[group])
+    return tiles
+
+
+def pack_early_kernel(lat_ref, lon_ref, fields_ref, flat_ref, first_ref, second_side_ref, first_side_ref):
+    read = plane_reader(fields_ref, flat_ref)
+    lat_even, lon_even = lat_ref[0] % 2 == 0, lon_ref[0] % 2 == 0
+
+    def early(plane):
+        own, halo = read(plane, 0, ROWS), first_ref[plane]
+        top = jnp.where(lat_even, own[:HALO], halo)
+        middle = jnp.where(lat_even, own[HALO:], own[:HALO])
+        return jnp.concatenate([top, middle, jnp.where(lat_even, halo, own[HALO:])], axis=0)
+
+    for ref, shift in (
+        (second_side_ref, jnp.where(lon_even, 0, HALO)), (first_side_ref, jnp.where(lon_even, HALO, 0))
+    ):
+        for group, tile in enumerate(side_tiles(EARLY, early, shift)):
+            ref[group, pl.ds(0, EARLY), :] = tile
     for group in range(GROUPS):
-        even = lon_ref[0] % 2 == 0
-        to_second_ref[group] = jnp.where(even, west[group], east[group])
-        to_first_ref[group] = jnp.where(even, east[group], west[group])
+        for row in range(EARLY, SPARE, 8):
+            second_side_ref[group, pl.ds(row, 8), :] = jnp.zeros((8, LANES), jnp.float32)
+
+
+def pack_late_kernel(lon_ref, second_ref, second_early_ref, first_early_ref, second_side_ref, first_side_ref):
+    lon_even = lon_ref[0] % 2 == 0
+    for out_ref, early_ref, shift in (
+        (second_side_ref, second_early_ref, jnp.where(lon_even, 0, HALO)),
+        (first_side_ref, first_early_ref, jnp.where(lon_even, HALO, 0)),
+    ):
+        for group, tile in enumerate(side_tiles(HALO, lambda plane: second_ref[plane], shift)):
+            out_ref[group, pl.ds(0, EARLY), :] = early_ref[group, pl.ds(0, EARLY), :]
+            out_ref[group, pl.ds(EARLY, HALO), :] = tile
 
 
 def joiner(lat_ref):
@@ -298,19 +325,37 @@
 
 
 def strips_kernel(
-    lat_ref, lon_ref, fields_ref, flat_ref, second_ref, first_ref, second_side_ref, first_side_ref, block_ref, out_ref, *scratch
+    lat_ref, lon_ref, fields_ref, flat_ref, second_ref, first_ref, sent_ref, early_ref, second_side_ref, first_side_ref, block_ref,
+    out_ref, *scratch, lat_count, lon_count,
 ):
     read, joined = plane_reader(fields_ref, flat_ref), joiner(lat_ref)
     lanes = lane_ids(EXT)
     upper = lanes >= 64
     place = lanes % 64
+    lat, lon = lat_ref[0], lon_ref[0]
+    lat_even, lon_even = lat % 2 == 0, lon % 2 == 0
 
     def ext(plane):
         return joined(first_ref[plane], read(plane, 0, ROWS), second_ref[plane])
 
-    even = lon_ref[0] % 2 == 0
-    from_west = [jnp.where(even, second_side_ref[group], first_side_ref[group]) for group in range(GROUPS)]
-    from_east = [jnp.where(even, first_side_ref[group], second_side_ref[group]) for group in range(GROUPS)]
+    other = (jnp.where(lon_even, lon - 1, lon + 1) + lon_count) % lon_count
+    seam = (lat == lat_count - 1) & (other == lon_count - 1 - lon)
+    back = lane_ids(HALO) + 7 - 2 * (lane_ids(HALO) % 8)
+
+    def in_order(value):
+        early, late = value[:EARLY], value[EARLY:]
+        return jnp.where(lat_even, jnp.concatenate([late, early], axis=0), jnp.concatenate([early, late], axis=0))
+
+    from_west, from_east = [], []
+    for group in range(GROUPS):
+        index = 8 * group + lane_ids(HALO) % 64 // 8
+        sign = jnp.where((index >= 2 * PAIRS) & (index < 4 * PAIRS), -1.0, 1.0)
+        own = sign * folded(sent_ref[group, pl.ds(2 * HALO, HALO), :], back)
+        at_seam = jnp.concatenate([early_ref[group, pl.ds(0, EARLY), :], own], axis=0)
+        second = in_order(jnp.where(seam, at_seam, second_side_ref[group]))
+        first = in_order(first_side_ref[group])
+        from_west.append(jnp.where(lon_even, second, first))
+        from_east.append(jnp.where(lon_even, first, second))
 
     def strip(index, low, high):
         group, slot = divmod(index, 8)
@@ -379,9 +424,12 @@
             lat_second.append((index_of(i, j), index_of(i, other_side(j))))
     lon_first = [(index_of(i, j), index_of(i ^ 1, j)) for i, j in everywhere]
     lon_second = [(index_of(i, j), index_of(other_side(i), j)) for i, j in everywhere]
+    at_seam = [j == lat_count - 1 and other_side(i) % lon_count == lon_count - 1 - i for i, j in everywhere]
+    lon_early = [pair for pair, seam in zip(lon_second, at_seam, strict=True) if seam]
+    lon_late = [pair for pair, seam in zip(lon_second, at_seam, strict=True) if not seam]
 
     flat = jnp.stack([bottom_level.astype(jnp.float32), coriolis])
-    rows_message, side_message = f32(PLANES, HALO, LANES), f32(GROUPS, EXT, LANES)
+    rows_message = f32(PLANES, HALO, LANES)
     held = (
         pltpu.VMEM((COMPS, LEVELS, HALO, LANES), jnp.float32), pltpu.VMEM((HALO, LANES), jnp.int32),
         pltpu.VMEM((HALO, LANES), jnp.float32), pltpu.SemaphoreType.DMA((3,)),
@@ -393,16 +441,21 @@
     second = lax.ppermute(to_second, axes, lat_second)
     to_first = call(pack_first_kernel, rows_message, (), 10**5, 10**6, lat, fields, flat)
     first = lax.ppermute(to_first, axes, lat_first)
+    to_second_early, to_first_early = call(
+        pack_early_kernel, (f32(GROUPS, SPARE, LANES), f32(GROUPS, EARLY, LANES)), (), 10**5, 10**6,
+        lat, lon, fields, flat, first,
+    )
+    early = lax.ppermute(to_second_early, axes, lon_early)
     to_second_side, to_first_side = call(
-        pack_sides_kernel, (side_message,) * 2, (), 10**5, 10**6, lat, lon, fields, flat, second, first
-    )
-    second_side = lax.ppermute(to_second_side, axes, lon_second)
+        pack_late_kernel, (f32(GROUPS, EXT, LANES),) * 2, (), 10**5, 10**6, lon, second, to_second_early, to_first_early
+    )
+    second_side = lax.ppermute(to_second_side, axes, lon_late)
     first_side = lax.ppermute(to_first_side, axes, lon_first)
     result = f32(COMPS, LEVELS, ROWS, LANES)
     block = call(block_kernel, result, scratch_for(LEVELS), 10**9, 10**6, lat, fields, flat, second, first)
     return call(
-        strips_kernel, result, scratch_for(PAIRS), 10**8, 10**6,
-        lat, lon, fields, flat, second, first, second_side, first_side, block,
+        functools.partial(strips_kernel, lat_count=lat_count, lon_count=lon_count), result, scratch_for(PAIRS), 10**8, 10**6,
+        lat, lon, fields, flat, second, first, to_second_early, early, second_side, first_side, block,
     )
 
 

time: 39 us -> 33.5 us (0.86)
  starting transfers between devices: 23.5 us -> 20.6 us
  waiting for transfers between devices: 6.69 us -> 4.03 us
    ppermute x1 -> x2, starting transfers between devices: 6.98 us -> 2.96 us  [the longest x1 2.3 us: local(): early = lax.ppermute(to_second_early, axes, lon_early)]
    ppermute x1, waiting for transfers between devices: 5.31 us -> 2.65 us  [local(): second = lax.ppermute(to_second, axes, lat_second)]
    ppermute x1, starting transfers between devices: 1.92 us -> 3 us  [local(): first_side = lax.ppermute(to_first_side, axes, lon_first)]
    pallas_call x5 -> x6, Pallas kernels: 8.41 us -> 8.5 us  [call(): pl.pallas_call(kernel, out_shape=out_shape, in_specs=[pl.BlockSpec(memory...]
  transfers between devices with their start and end apart: 4 -> 5, of which waited for: 2 -> 2; matrix products, arithmetic and copies ran while one was open for 0% -> 0% of each run, Pallas kernels for 8% -> 10%
where the time goes in v3:
time: 33.5 us; the launch traced here: 33.3 us
  starting transfers between devices  20.6 us (61%)
  Pallas kernels  8.5 us (25%)
  waiting for transfers between devices  4.03 us (12%)
    ppermute x1, starting transfers between devices, local(): second = lax.ppermute(to_second, axes, lat_second)  12.7 us
    pallas_call x6, Pallas kernels, call(): pl.pallas_call(kernel, out_shape=out_shape, in_specs=[pl.BlockSpec(memory...  8.5 us
    ppermute x1, starting transfers between devices, local(): first_side = lax.ppermute(to_first_side, axes, lon_first)  3 us
    ppermute x1, waiting for transfers between devices, local(): second = lax.ppermute(to_second, axes, lat_second)  2.65 us
    ppermute x1, starting transfers between devices, local(): early = lax.ppermute(to_second_early, axes, lon_early)  2.3 us
    ppermute x1, starting transfers between devices, local(): first = lax.ppermute(to_first, axes, lat_first)  1.92 us
    ppermute x1, waiting for transfers between devices, local(): first = lax.ppermute(to_first, axes, lat_first)  1.37 us
  transfers between devices with their start and end apart: 5, of which 2 were waited for; matrix products, arithmetic and copies ran while one was open for 0% of the time, Pallas kernels for 10%

profile of v3, /device:TPU:27, one launch (start us, length us, event | category | flops | bytes accessed | tf_op | source)
XLA Modules:
  0.0 33.3 jit_solution(12878531959871804558)
XLA Ops:
  0.0 0.0 copy-start
  0.0 0.0 copy-start.1
  0.0 1.8 %shard_map.37 = f32[43,8,128]{2,1,0:T(8,128)} custom-call(s32[1]{0:T(128)} %bitcast.lat_ref, f32[4,10,16,128]{3,2,1,0:T(8,128)} %fields_ref.7, s32[16,128]{1,0:T(8,128)} %bottom_any.1, f32[16,128]{1,0:T(8,128)} %coriolis_any.1), custom_call_target="tpu_custom_call" | custom-call | flops 100000 | bytes 1000000 | tf_op jit(solution)/shard_map/pallas_call | solution.py:389
  1.8 0.0 copy-start.2
  1.8 12.7 %collective-permute-start = (f32[43,8,128]{2,1,0:T(8,128)}, f32[43,8,128]{2,1,0:T(8,128)S(1)}, u32[]{:S(2)}, u32[]{:S(2)}) collective-permute-start(f32[43,8,128]{2,1,0:T(8,128)} %shard_map.37), channel_id=1, source_target_pairs={{1,2},{2,1},{3,4},{4,3},{5,6},{6,5},{7,8},{8,7},{9,10},{10,9},{11,... | collective-permute-start | bytes 528392 | tf_op jit(solution)/shard_map/ppermute | solution.py:441
  14.5 0.0 copy-done.1
  14.5 0.0 copy-done.2
  14.6 0.0 copy-done
  14.6 1.9 %collective-permute-start.1 = (f32[42,8,128]{2,1,0:T(8,128)S(1)}, f32[42,8,128]{2,1,0:T(8,128)S(1)}, u32[]{:S(2)}, u32[]{:S(2)}) collective-permute-start(f32[42,8,128]{2,1,0:T(8,128)S(1)} %shard_map.38), channel_id=1, source_target_pairs={{0,1},{1,0},{2,3},{3,2},{4,5},{5,4},{6,7},{7,6},{8,9},{9,8},{10,11... | collective-permute-start | bytes 516104 | tf_op jit(solution)/shard_map/ppermute | solution.py:443
  16.5 1.4 %collective-permute-done.1.first_ref = f32[42,8,128]{2,1,0:T(8,128)S(1)} collective-permute-done((f32[42,8,128]{2,1,0:T(8,128)S(1)}, f32[42,8,128]{2,1,0:T(8,128)S(1)}, u32[]{:S(2)}, u32[]{:S(2)}) %collective-permute-start.1) | collective-permute-done | bytes 172064 | tf_op jit(solution)/shard_map/ppermute | solution.py:443
  17.9 0.4 %shard_map.39 = (f32[3,48,128]{2,1,0:T(8,128)S(1)}, f32[3,24,128]{2,1,0:T(8,128)S(1)}) custom-call(s32[1]{0:T(128)} %bitcast.lat_ref, s32[1]{0:T(128)} %bitcast.1.lon_ref, f32[4,10,16,128]{3,2,1,0:T(8,128)S(1)} %copy-done, f32[2,16,128]{2,1,0:T(8,128)S(1)} %pad_maximum_fusion.flat_ref, f32[42,8,128]{2,1,0:T(8,128)S(1)} %collective-permute-done.1.first_ref), custom_call_target="tpu_custom_call" | custom-call | flops 100000 | bytes 1000000 | tf_op jit(solution)/shard_map/pallas_call | solution.py:389
  18.3 2.3 %collective-permute-start.2 = (f32[3,48,128]{2,1,0:T(8,128)S(1)}, f32[3,48,128]{2,1,0:T(8,128)S(1)}, u32[]{:S(2)}, u32[]{:S(2)}) collective-permute-start(f32[3,48,128]{2,1,0:T(8,128)S(1)} %get-tuple-element.9.second_early_ref.sent_ref), channel_id=1, source_target_pairs={{15,511},{255,271},{271,255},{511,15}} | collective-permute-start | bytes 221192 | tf_op jit(solution)/shard_map/ppermute | solution.py:448
  20.6 2.6 %collective-permute-done.second_ref = f32[43,8,128]{2,1,0:T(8,128)S(1)} collective-permute-done((f32[43,8,128]{2,1,0:T(8,128)}, f32[43,8,128]{2,1,0:T(8,128)S(1)}, u32[]{:S(2)}, u32[]{:S(2)}) %collective-permute-start) | collective-permute-done | bytes 176160 | tf_op jit(solution)/shard_map/ppermute | solution.py:441
  23.2 0.2 shard_map.40
  23.4 0.7 %collective-permute-start.3 = (f32[3,32,128]{2,1,0:T(8,128)S(1)}, f32[3,32,128]{2,1,0:T(8,128)S(1)}, u32[]{:S(2)}, u32[]{:S(2)}) collective-permute-start(f32[3,32,128]{2,1,0:T(8,128)S(1)} %get-tuple-element.11), channel_id=1, source_target_pairs={{0,496},{1,497},{2,498},{3,499},{4,500},{5,501},{6,502},{7,503},{8... | collective-permute-start | bytes 147464 | tf_op jit(solution)/shard_map/ppermute | solution.py:452
  24.1 3.0 %collective-permute-start.4 = (f32[3,32,128]{2,1,0:T(8,128)S(1)}, f32[3,32,128]{2,1,0:T(8,128)S(1)}, u32[]{:S(2)}, u32[]{:S(2)}) collective-permute-start(f32[3,32,128]{2,1,0:T(8,128)S(1)} %get-tuple-element.12), channel_id=1, source_target_pairs={{0,16},{1,17},{2,18},{3,19},{4,20},{5,21},{6,22},{7,23},{8,24},{9,... | collective-permute-start | bytes 147464 | tf_op jit(solution)/shard_map/ppermute | solution.py:453
  27.1 2.9 %shard_map.41.block_ref = f32[4,10,16,128]{3,2,1,0:T(8,128)S(1)} custom-call(s32[1]{0:T(128)} %bitcast.lat_ref, f32[4,10,16,128]{3,2,1,0:T(8,128)S(1)} %copy-done, f32[2,16,128]{2,1,0:T(8,128)S(1)} %pad_maximum_fusion.flat_ref, f32[43,8,128]{2,1,0:T(8,128)S(1)} %collective-permute-done.second_ref, f32[42,8,128]{2,1,0:T(8,128)S(1)} %collective-permute-done.1.first_ref), custom_call_target="tpu_custom_call" | custom-call | flops 1000000000 | bytes 1000000 | tf_op jit(solution)/shard_map/pallas_call | solution.py:389
  30.0 0.0 collective-permute-done.3.second_side_ref
  30.0 0.0 collective-permute-done.4.first_side_ref
  30.0 0.0 collective-permute-done.2.early_ref
  30.0 3.2 %shard_map.42 = f32[4,10,16,128]{3,2,1,0:T(8,128)} custom-call(s32[1]{0:T(128)} %bitcast.lat_ref, s32[1]{0:T(128)} %bitcast.1.lon_ref, f32[4,10,16,128]{3,2,1,0:T(8,128)S(1)} %copy-done, f32[2,16,128]{2,1,0:T(8,128)S(1)} %pad_maximum_fusion.flat_ref, f32[43,8,128]{2,1,0:T(8,128)S(1)} %collective-permute-done.second_ref, ...), custom_call_target="tpu_custom_call" | custom-call | flops 100000000 | bytes 1000000 | tf_op jit(solution)/shard_map/pallas_call | solution.py:389
  (3 shorter events, 0.0 us)
Async XLA Ops:
  0.0 14.6 %copy-start = (f32[4,10,16,128]{3,2,1,0:T(8,128)S(1)}, f32[4,10,16,128]{3,2,1,0:T(8,128)}, u32[]{:S(2)}) copy-start(f32[4,10,16,128]{3,2,1,0:T(8,128)} %fields_ref.7) | copy-start | bytes 983044
  0.0 14.5 %copy-start.1 = (s32[16,128]{1,0:T(8,128)S(1)}, s32[16,128]{1,0:T(8,128)}, u32[]{:S(2)}) copy-start(s32[16,128]{1,0:T(8,128)} %bottom_any.1) | copy-start | bytes 24580
  1.8 12.7 %copy-start.2 = (f32[16,128]{1,0:T(8,128)S(1)}, f32[16,128]{1,0:T(8,128)}, u32[]{:S(2)}) copy-start(f32[16,128]{1,0:T(8,128)} %coriolis_any.1) | copy-start | bytes 24580
  1.8 21.4 %collective-permute-start = (f32[43,8,128]{2,1,0:T(8,128)}, f32[43,8,128]{2,1,0:T(8,128)S(1)}, u32[]{:S(2)}, u32[]{:S(2)}) collective-permute-start(f32[43,8,128]{2,1,0:T(8,128)} %shard_map.37), channel_id=1, source_target_pairs={{1,2},{2,1},{3,4},{4,3},{5,6},{6,5},{7,8},{8,7},{9,10},{10,9},{11,... | collective-permute-start | bytes 528392 | tf_op jit(solution)/shard_map/ppermute | solution.py:441
  14.6 3.3 %collective-permute-start.1 = (f32[42,8,128]{2,1,0:T(8,128)S(1)}, f32[42,8,128]{2,1,0:T(8,128)S(1)}, u32[]{:S(2)}, u32[]{:S(2)}) collective-permute-start(f32[42,8,128]{2,1,0:T(8,128)S(1)} %shard_map.38), channel_id=1, source_target_pairs={{0,1},{1,0},{2,3},{3,2},{4,5},{5,4},{6,7},{7,6},{8,9},{9,8},{10,11... | collective-permute-start | bytes 516104 | tf_op jit(solution)/shard_map/ppermute | solution.py:443
  18.3 11.8 %collective-permute-start.2 = (f32[3,48,128]{2,1,0:T(8,128)S(1)}, f32[3,48,128]{2,1,0:T(8,128)S(1)}, u32[]{:S(2)}, u32[]{:S(2)}) collective-permute-start(f32[3,48,128]{2,1,0:T(8,128)S(1)} %get-tuple-element.9.second_early_ref.sent_ref), channel_id=1, source_target_pairs={{15,511},{255,271},{271,255},{511,15}} | collective-permute-start | bytes 221192 | tf_op jit(solution)/shard_map/ppermute | solution.py:448
  23.4 6.6 %collective-permute-start.3 = (f32[3,32,128]{2,1,0:T(8,128)S(1)}, f32[3,32,128]{2,1,0:T(8,128)S(1)}, u32[]{:S(2)}, u32[]{:S(2)}) collective-permute-start(f32[3,32,128]{2,1,0:T(8,128)S(1)} %get-tuple-element.11), channel_id=1, source_target_pairs={{0,496},{1,497},{2,498},{3,499},{4,500},{5,501},{6,502},{7,503},{8... | collective-permute-start | bytes 147464 | tf_op jit(solution)/shard_map/ppermute | solution.py:452
  24.1 6.0 %collective-permute-start.4 = (f32[3,32,128]{2,1,0:T(8,128)S(1)}, f32[3,32,128]{2,1,0:T(8,128)S(1)}, u32[]{:S(2)}, u32[]{:S(2)}) collective-permute-start(f32[3,32,128]{2,1,0:T(8,128)S(1)} %get-tuple-element.12), channel_id=1, source_target_pairs={{0,16},{1,17},{2,18},{3,19},{4,20},{5,21},{6,22},{7,23},{8,24},{9,... | collective-permute-start | bytes 147464 | tf_op jit(solution)/shard_map/ppermute | solution.py:453

commit v4 on v3

--- a/solution.py
+++ b/solution.py
@@ -28,7 +28,6 @@
 LANES = 128
 BATCH = 5
 LAG = 1
-LIMIT = 56
 GROUPS = 3
 
 
@@ -90,45 +89,6 @@
     return jnp.take_along_axis(jnp.take_along_axis(value, lanes, axis=1), rows, axis=0)
 
 
-def pack_second_kernel(
-    lat_ref, fields_any, bottom_any, coriolis_any, second_ref, rows_ref, bottom_ref, coriolis_ref, semaphores, *, lat_count
-):
-    lat = lat_ref[0]
-    row = pl.multiple_of(jnp.where(lat % 2 == 0, 0, HALO), HALO)
-    here = pl.ds(row, HALO)
-    copies = [
-        pltpu.make_async_copy(source, target, semaphores.at[index])
-        for index, (source, target) in enumerate((
-            (fields_any.at[:, :, here, :], rows_ref),
-            (bottom_any.at[here, :], bottom_ref),
-            (coriolis_any.at[here, :], coriolis_ref),
-        ))
-    ]
-    for copy in copies:
-        copy.start()
-    for copy in copies:
-        copy.wait()
-
-    def read(plane):
-        if plane < COMPS * LEVELS:
-            return rows_ref[plane // LEVELS, plane % LEVELS]
-        return bottom_ref[...].astype(jnp.float32) if plane == PLANES - 2 else coriolis_ref[...]
-
-    second_ref[PLANES] = jnp.zeros((HALO, LANES), jnp.float32)
-
-    @pl.when(lat < lat_count - 1)
-    def _():
-        for plane in range(PLANES):
-            second_ref[plane] = read(plane)
-
-    @pl.when(lat == lat_count - 1)
-    def _():
-        back = LANES - 1 - lane_ids(HALO)
-        for plane in range(PLANES):
-            value = folded(read(plane), back)
-            second_ref[plane] = -value if 2 * LEVELS <= plane < 4 * LEVELS else value
-
-
 def pack_first_kernel(lat_ref, fields_ref, flat_ref, first_ref):
     read = plane_reader(fields_ref, flat_ref)
     row = pl.multiple_of(jnp.where(lat_ref[0] % 2 == 0, HALO, 0), HALO)
@@ -167,8 +127,23 @@
             second_side_ref[group, pl.ds(row, 8), :] = jnp.zeros((8, LANES), jnp.float32)
 
 
-def pack_late_kernel(lon_ref, second_ref, second_early_ref, first_early_ref, second_side_ref, first_side_ref):
-    lon_even = lon_ref[0] % 2 == 0
+def pack_late_kernel(
+    lat_ref, lon_ref, received_ref, second_early_ref, first_early_ref, second_ref, second_side_ref, first_side_ref, *, lat_count
+):
+    lat, lon_even = lat_ref[0], lon_ref[0] % 2 == 0
+
+    @pl.when(lat < lat_count - 1)
+    def _():
+        for plane in range(PLANES):
+            second_ref[plane] = received_ref[plane]
+
+    @pl.when(lat == lat_count - 1)
+    def _():
+        back = LANES - 1 - lane_ids(HALO)
+        for plane in range(PLANES):
+            value = folded(received_ref[plane], back)
+            second_ref[plane] = -value if 2 * LEVELS <= plane < 4 * LEVELS else value
+
     for out_ref, early_ref, shift in (
         (second_side_ref, second_early_ref, jnp.where(lon_even, 0, HALO)),
         (first_side_ref, first_early_ref, jnp.where(lon_even, HALO, 0)),
@@ -383,16 +358,15 @@
     )
 
 
-def call(kernel, out_shape, scratch, flops, moved, *operands, whole=False):
-    far = pltpu.HBM if whole else pltpu.VMEM
-    places = [pltpu.SMEM if operand.shape == (1,) else far for operand in operands]
+def call(kernel, out_shape, scratch, flops, moved, *operands):
+    places = [pltpu.SMEM if operand.shape == (1,) else pltpu.VMEM for operand in operands]
     return pl.pallas_call(
         kernel,
         out_shape=out_shape,
         in_specs=[pl.BlockSpec(memory_space=place) for place in places],
         out_specs=jax.tree.map(lambda _: pl.BlockSpec(memory_space=pltpu.VMEM), out_shape),
         scratch_shapes=scratch,
-        compiler_params=pltpu.CompilerParams(vmem_limit_bytes=(LIMIT if whole else 24) << 20),
+        compiler_params=pltpu.CompilerParams(vmem_limit_bytes=24 << 20),
         cost_estimate=pl.CostEstimate(flops=flops, bytes_accessed=moved, transcendentals=0),
     )(*operands)
 
@@ -429,16 +403,22 @@
     lon_late = [pair for pair, seam in zip(lon_second, at_seam, strict=True) if not seam]
 
     flat = jnp.stack([bottom_level.astype(jnp.float32), coriolis])
+
+    def half(value, dim, even):
+        return jnp.where(
+            even, lax.slice_in_dim(value, 0, HALO, axis=dim), lax.slice_in_dim(value, HALO, ROWS, axis=dim)
+        )
+
+    even = lat[0] % 2 == 0
+    rows, even = lax.optimization_barrier((half(fields, 2, even), even))
     rows_message = f32(PLANES, HALO, LANES)
-    held = (
-        pltpu.VMEM((COMPS, LEVELS, HALO, LANES), jnp.float32), pltpu.VMEM((HALO, LANES), jnp.int32),
-        pltpu.VMEM((HALO, LANES), jnp.float32), pltpu.SemaphoreType.DMA((3,)),
-    )
-    to_second = call(
-        functools.partial(pack_second_kernel, lat_count=lat_count), f32(PLANES + 1, HALO, LANES), held, 10**5, 10**6,
-        lat, fields, bottom_level, coriolis, whole=True,
-    )
-    second = lax.ppermute(to_second, axes, lat_second)
+    to_second = jnp.concatenate([
+        rows.reshape(COMPS * LEVELS, HALO, LANES),
+        half(bottom_level, 0, even).astype(jnp.float32)[None],
+        half(coriolis, 0, even)[None],
+        jnp.zeros((1, HALO, LANES), jnp.float32),
+    ])
+    received = lax.ppermute(to_second, axes, lat_second)
     to_first = call(pack_first_kernel, rows_message, (), 10**5, 10**6, lat, fields, flat)
     first = lax.ppermute(to_first, axes, lat_first)
     to_second_early, to_first_early = call(
@@ -446,8 +426,9 @@
         lat, lon, fields, flat, first,
     )
     early = lax.ppermute(to_second_early, axes, lon_early)
-    to_second_side, to_first_side = call(
-        pack_late_kernel, (f32(GROUPS, EXT, LANES),) * 2, (), 10**5, 10**6, lon, second, to_second_early, to_first_early
+    second, to_second_side, to_first_side = call(
+        functools.partial(pack_late_kernel, lat_count=lat_count), (rows_message,) + (f32(GROUPS, EXT, LANES),) * 2, (),
+        10**5, 10**6, lat, lon, received, to_second_early, to_first_early,
     )
     second_side = lax.ppermute(to_second_side, axes, lon_late)
     first_side = lax.ppermute(to_first_side, axes, lon_first)

time: 33.5 us -> 32.9 us (0.982)
  the two profiles are of different devices: /device:TPU:27 before, /device:TPU:2 now
where the time goes in v4:
time: 32.9 us; the launch traced here: 32.7 us
  starting transfers between devices  22 us (67%)
  Pallas kernels  6.7 us (20%)
  waiting for transfers between devices  2.64 us (8%)
  other arithmetic  1.17 us (4%)
    ppermute x1, starting transfers between devices, local(): second_side = lax.ppermute(to_second_side, axes, lon_late)  13.1 us
    pallas_call x5, Pallas kernels, call(): pl.pallas_call(kernel, out_shape=out_shape, in_specs=[pl.BlockSpec(memory...  6.7 us
    ppermute x1, starting transfers between devices, local(): received = lax.ppermute(to_second, axes, lat_second)  4.33 us
    ppermute x1, starting transfers between devices, local(): first = lax.ppermute(to_first, axes, lat_first)  1.92 us
    ppermute x1, starting transfers between devices, local(): first_side = lax.ppermute(to_first_side, axes, lon_first)  1.92 us
    ppermute x1, waiting for transfers between devices, local(): first = lax.ppermute(to_first, axes, lat_first)  1.37 us
    ppermute x1, waiting for transfers between devices, local(): first_side = lax.ppermute(to_first_side, axes, lon_first)  1.12 us
    select_n x1, other arithmetic, half(): jnp.where(even, lax.slice_in_dim(value, 0, HALO, axis=dim), lax.slice_in_...  1.04 us
  transfers between devices with their start and end apart: 5, of which 3 were waited for; matrix products, arithmetic and copies ran while one was open for 0% of the time, Pallas kernels for 11%

profile of v4, /device:TPU:2, one launch (start us, length us, event | category | flops | bytes accessed | tf_op | source)
XLA Modules:
  0.0 32.7 jit_solution(12644076856625434487)
XLA Ops:
  0.0 0.0 copy-start.2
  0.0 0.0 copy-start.1
  0.0 1.0 %slice_select_fusion = f32[4,10,8,128]{3,2,1,0:T(8,128)S(1)} fusion(f32[4,10,16,128]{3,2,1,0:T(8,128)} %fields_ref.7, pred[]{:T(512)S(6)} %eq.5), kind=kLoop, calls=%fused_computation.1 | loop fusion | flops 40960 | bytes 491521 | tf_op jit(solution)/shard_map/jit(_where)/select_n | solution.py:408
  1.0 0.0 copy-done.2
  1.1 0.0 copy-start
  1.1 0.0 copy-done.1
  1.1 0.1 pad.3.clone
  1.2 0.1 maximum_maximum_fusion
  1.3 4.3 %collective-permute-start = (f32[43,8,128]{2,1,0:T(8,128)S(1)}, f32[43,8,128]{2,1,0:T(8,128)S(1)}, u32[]{:S(2)}, u32[]{:S(2)}) collective-permute-start(f32[43,8,128]{2,1,0:T(8,128)S(1)} %maximum_maximum_fusion), channel_id=1, source_target_pairs={{1,2},{2,1},{3,4},{4,3},{5,6},{6,5},{7,8},{8,7},{9,10},{10,9},{11,... | collective-permute-start | bytes 528392 | tf_op jit(solution)/shard_map/ppermute | solution.py:421
  5.7 0.0 copy-done
  5.7 1.9 %collective-permute-start.1 = (f32[42,8,128]{2,1,0:T(8,128)S(1)}, f32[42,8,128]{2,1,0:T(8,128)S(1)}, u32[]{:S(2)}, u32[]{:S(2)}) collective-permute-start(f32[42,8,128]{2,1,0:T(8,128)S(1)} %shard_map.37), channel_id=1, source_target_pairs={{0,1},{1,0},{2,3},{3,2},{4,5},{5,4},{6,7},{7,6},{8,9},{9,8},{10,11... | collective-permute-start | bytes 516104 | tf_op jit(solution)/shard_map/ppermute | solution.py:423
  7.6 1.4 %collective-permute-done.1.first_ref = f32[42,8,128]{2,1,0:T(8,128)S(1)} collective-permute-done((f32[42,8,128]{2,1,0:T(8,128)S(1)}, f32[42,8,128]{2,1,0:T(8,128)S(1)}, u32[]{:S(2)}, u32[]{:S(2)}) %collective-permute-start.1) | collective-permute-done | bytes 172064 | tf_op jit(solution)/shard_map/ppermute | solution.py:423
  9.0 0.4 %shard_map.38 = (f32[3,48,128]{2,1,0:T(8,128)S(1)}, f32[3,24,128]{2,1,0:T(8,128)S(1)}) custom-call(s32[1]{0:T(128)} %bitcast.lat_ref, s32[1]{0:T(128)} %bitcast.1.lon_ref, f32[4,10,16,128]{3,2,1,0:T(8,128)S(1)} %copy-done, f32[2,16,128]{2,1,0:T(8,128)S(1)} %pad_maximum_fusion.flat_ref, f32[42,8,128]{2,1,0:T(8,128)S(1)} %collective-permute-done.1.first_ref), custom_call_target="tpu_custom_call" | custom-call | flops 100000 | bytes 1000000 | tf_op jit(solution)/shard_map/pallas_call | solution.py:363
  9.4 0.7 %collective-permute-start.2 = (f32[3,48,128]{2,1,0:T(8,128)S(1)}, f32[3,48,128]{2,1,0:T(8,128)S(1)}, u32[]{:S(2)}, u32[]{:S(2)}) collective-permute-start(f32[3,48,128]{2,1,0:T(8,128)S(1)} %get-tuple-element.14.second_early_ref.sent_ref), channel_id=1, source_target_pairs={{15,511},{255,271},{271,255},{511,15}} | collective-permute-start | bytes 221192 | tf_op jit(solution)/shard_map/ppermute | solution.py:428
  10.0 0.1 collective-permute-done.received_ref
  10.2 0.2 shard_map.39
  10.4 13.1 %collective-permute-start.3 = (f32[3,32,128]{2,1,0:T(8,128)S(1)}, f32[3,32,128]{2,1,0:T(8,128)S(1)}, u32[]{:S(2)}, u32[]{:S(2)}) collective-permute-start(f32[3,32,128]{2,1,0:T(8,128)S(1)} %get-tuple-element.17), channel_id=1, source_target_pairs={{0,496},{1,497},{2,498},{3,499},{4,500},{5,501},{6,502},{7,503},{8... | collective-permute-start | bytes 147464 | tf_op jit(solution)/shard_map/ppermute | solution.py:433
  23.5 1.9 %collective-permute-start.4 = (f32[3,32,128]{2,1,0:T(8,128)S(1)}, f32[3,32,128]{2,1,0:T(8,128)S(1)}, u32[]{:S(2)}, u32[]{:S(2)}) collective-permute-start(f32[3,32,128]{2,1,0:T(8,128)S(1)} %get-tuple-element.18), channel_id=1, source_target_pairs={{0,16},{1,17},{2,18},{3,19},{4,20},{5,21},{6,22},{7,23},{8,24},{9,... | collective-permute-start | bytes 147464 | tf_op jit(solution)/shard_map/ppermute | solution.py:434
  25.4 2.9 %shard_map.40.block_ref = f32[4,10,16,128]{3,2,1,0:T(8,128)S(1)} custom-call(s32[1]{0:T(128)} %bitcast.lat_ref, f32[4,10,16,128]{3,2,1,0:T(8,128)S(1)} %copy-done, f32[2,16,128]{2,1,0:T(8,128)S(1)} %pad_maximum_fusion.flat_ref, f32[42,8,128]{2,1,0:T(8,128)S(1)} %get-tuple-element.16.second_ref, f32[42,8,128]{2,1,0:T(8,128)S(1)} %collective-permute-done.1.first_ref), custom_call_target="tpu_custom_call" | custom-call | flops 1000000000 | bytes 1000000 | tf_op jit(solution)/shard_map/pallas_call | solution.py:363
  28.3 0.0 collective-permute-done.3.second_side_ref
  28.4 1.1 %collective-permute-done.4.first_side_ref = f32[3,32,128]{2,1,0:T(8,128)S(1)} collective-permute-done((f32[3,32,128]{2,1,0:T(8,128)S(1)}, f32[3,32,128]{2,1,0:T(8,128)S(1)}, u32[]{:S(2)}, u32[]{:S(2)}) %collective-permute-start.4) | collective-permute-done | bytes 49184 | tf_op jit(solution)/shard_map/ppermute | solution.py:434
  29.5 0.0 collective-permute-done.2.early_ref
  29.5 3.2 %shard_map.41 = f32[4,10,16,128]{3,2,1,0:T(8,128)} custom-call(s32[1]{0:T(128)} %bitcast.lat_ref, s32[1]{0:T(128)} %bitcast.1.lon_ref, f32[4,10,16,128]{3,2,1,0:T(8,128)S(1)} %copy-done, f32[2,16,128]{2,1,0:T(8,128)S(1)} %pad_maximum_fusion.flat_ref, f32[42,8,128]{2,1,0:T(8,128)S(1)} %get-tuple-element.16.second_ref, ...), custom_call_target="tpu_custom_call" | custom-call | flops 100000000 | bytes 1000000 | tf_op jit(solution)/shard_map/pallas_call | solution.py:363
  (5 shorter events, 0.0 us)
Async XLA Ops:
  0.0 1.0 %copy-start.2 = (f32[16,128]{1,0:T(8,128)S(1)}, f32[16,128]{1,0:T(8,128)}, u32[]{:S(2)}) copy-start(f32[16,128]{1,0:T(8,128)} %param.6) | copy-start | bytes 24580
  0.0 1.1 %copy-start.1 = (s32[16,128]{1,0:T(8,128)S(1)}, s32[16,128]{1,0:T(8,128)}, u32[]{:S(2)}) copy-start(s32[16,128]{1,0:T(8,128)} %param.5) | copy-start | bytes 24580
  1.1 4.6 %copy-start = (f32[4,10,16,128]{3,2,1,0:T(8,128)S(1)}, f32[4,10,16,128]{3,2,1,0:T(8,128)}, u32[]{:S(2)}) copy-start(f32[4,10,16,128]{3,2,1,0:T(8,128)} %fields_ref.7) | copy-start | bytes 983044
  1.3 8.9 %collective-permute-start = (f32[43,8,128]{2,1,0:T(8,128)S(1)}, f32[43,8,128]{2,1,0:T(8,128)S(1)}, u32[]{:S(2)}, u32[]{:S(2)}) collective-permute-start(f32[43,8,128]{2,1,0:T(8,128)S(1)} %maximum_maximum_fusion), channel_id=1, source_target_pairs={{1,2},{2,1},{3,4},{4,3},{5,6},{6,5},{7,8},{8,7},{9,10},{10,9},{11,... | collective-permute-start | bytes 528392 | tf_op jit(solution)/shard_map/ppermute | solution.py:421
  5.7 3.3 %collective-permute-start.1 = (f32[42,8,128]{2,1,0:T(8,128)S(1)}, f32[42,8,128]{2,1,0:T(8,128)S(1)}, u32[]{:S(2)}, u32[]{:S(2)}) collective-permute-start(f32[42,8,128]{2,1,0:T(8,128)S(1)} %shard_map.37), channel_id=1, source_target_pairs={{0,1},{1,0},{2,3},{3,2},{4,5},{5,4},{6,7},{7,6},{8,9},{9,8},{10,11... | collective-permute-start | bytes 516104 | tf_op jit(solution)/shard_map/ppermute | solution.py:423
  9.4 20.1 %collective-permute-start.2 = (f32[3,48,128]{2,1,0:T(8,128)S(1)}, f32[3,48,128]{2,1,0:T(8,128)S(1)}, u32[]{:S(2)}, u32[]{:S(2)}) collective-permute-start(f32[3,48,128]{2,1,0:T(8,128)S(1)} %get-tuple-element.14.second_early_ref.sent_ref), channel_id=1, source_target_pairs={{15,511},{255,271},{271,255},{511,15}} | collective-permute-start | bytes 221192 | tf_op jit(solution)/shard_map/ppermute | solution.py:428
  10.4 18.0 %collective-permute-start.3 = (f32[3,32,128]{2,1,0:T(8,128)S(1)}, f32[3,32,128]{2,1,0:T(8,128)S(1)}, u32[]{:S(2)}, u32[]{:S(2)}) collective-permute-start(f32[3,32,128]{2,1,0:T(8,128)S(1)} %get-tuple-element.17), channel_id=1, source_target_pairs={{0,496},{1,497},{2,498},{3,499},{4,500},{5,501},{6,502},{7,503},{8... | collective-permute-start | bytes 147464 | tf_op jit(solution)/shard_map/ppermute | solution.py:433
  23.5 6.0 %collective-permute-start.4 = (f32[3,32,128]{2,1,0:T(8,128)S(1)}, f32[3,32,128]{2,1,0:T(8,128)S(1)}, u32[]{:S(2)}, u32[]{:S(2)}) collective-permute-start(f32[3,32,128]{2,1,0:T(8,128)S(1)} %get-tuple-element.18), channel_id=1, source_target_pairs={{0,16},{1,17},{2,18},{3,19},{4,20},{5,21},{6,22},{7,23},{8,24},{9,... | collective-permute-start | bytes 147464 | tf_op jit(solution)/shard_map/ppermute | solution.py:434

commit v5 on v4

--- a/solution.py
+++ b/solution.py
@@ -301,7 +301,7 @@
 
 def strips_kernel(
     lat_ref, lon_ref, fields_ref, flat_ref, second_ref, first_ref, sent_ref, early_ref, second_side_ref, first_side_ref, block_ref,
-    out_ref, *scratch, lat_count, lon_count,
+    out_any, out_ref, semaphores, *scratch, lat_count, lon_count,
 ):
     read, joined = plane_reader(fields_ref, flat_ref), joiner(lat_ref)
     lanes = lane_ids(EXT)
@@ -346,25 +346,32 @@
     bottom, twist = ext(PLANES - 2), ext(PLANES - 1)
     own_lanes = lane_ids(ROWS)
 
+    def leave(level):
+        return pltpu.make_async_copy(out_ref.at[:, level], out_any.at[:, level], semaphores.at[level])
+
     def finish(comp, slab, new):
         for half in range(2):
             level = slab + half * PAIRS
             value = block_ref[comp, level]
             value = jnp.where(own_lanes < 8, turned(-8 - 64 * half)(new), value)
             out_ref[comp, level] = jnp.where(own_lanes >= 120, turned(120 - 32 - 64 * half)(new), value)
+            if comp == COMPS - 1:
+                leave(level).start()
 
     evolve(
         scratch, PAIRS, True, plain_of, strip(COMPS * PAIRS, bottom, bottom), strip(COMPS * PAIRS + 1, twist, twist), finish
     )
-
-
-def call(kernel, out_shape, scratch, flops, moved, *operands):
+    for level in range(LEVELS):
+        leave(level).wait()
+
+
+def call(kernel, out_shape, scratch, flops, moved, *operands, out=pltpu.VMEM):
     places = [pltpu.SMEM if operand.shape == (1,) else pltpu.VMEM for operand in operands]
     return pl.pallas_call(
         kernel,
         out_shape=out_shape,
         in_specs=[pl.BlockSpec(memory_space=place) for place in places],
-        out_specs=jax.tree.map(lambda _: pl.BlockSpec(memory_space=pltpu.VMEM), out_shape),
+        out_specs=jax.tree.map(lambda _: pl.BlockSpec(memory_space=out), out_shape),
         scratch_shapes=scratch,
         compiler_params=pltpu.CompilerParams(vmem_limit_bytes=24 << 20),
         cost_estimate=pl.CostEstimate(flops=flops, bytes_accessed=moved, transcendentals=0),
@@ -435,8 +442,9 @@
     result = f32(COMPS, LEVELS, ROWS, LANES)
     block = call(block_kernel, result, scratch_for(LEVELS), 10**9, 10**6, lat, fields, flat, second, first)
     return call(
-        functools.partial(strips_kernel, lat_count=lat_count, lon_count=lon_count), result, scratch_for(PAIRS), 10**8, 10**6,
-        lat, lon, fields, flat, second, first, to_second_early, early, second_side, first_side, block,
+        functools.partial(strips_kernel, lat_count=lat_count, lon_count=lon_count), result,
+        (pltpu.VMEM(result.shape, jnp.float32), pltpu.SemaphoreType.DMA((LEVELS,))) + scratch_for(PAIRS), 10**8, 10**6,
+        lat, lon, fields, flat, second, first, to_second_early, early, second_side, first_side, block, out=pltpu.HBM,
     )
 
 

time: 32.9 us -> 32.9 us (level)
  the two profiles are of different devices: /device:TPU:2 before, /device:TPU:27 now
where the time goes in v5:
time: 32.9 us; the launch traced here: 32.7 us
  starting transfers between devices  20.7 us (63%)
  Pallas kernels  6.82 us (21%)
  waiting for transfers between devices  3.74 us (11%)
  other arithmetic  1.17 us (4%)
    ppermute x1, starting transfers between devices, local(): received = lax.ppermute(to_second, axes, lat_second)  12.7 us
    pallas_call x5, Pallas kernels, call(): pl.pallas_call(kernel, out_shape=out_shape, in_specs=[pl.BlockSpec(memory...  6.82 us
    ppermute x1, starting transfers between devices, local(): first_side = lax.ppermute(to_first_side, axes, lon_first)  3 us
    ppermute x1, starting transfers between devices, local(): early = lax.ppermute(to_second_early, axes, lon_early)  2.4 us
    ppermute x1, waiting for transfers between devices, local(): received = lax.ppermute(to_second, axes, lat_second)  2.36 us
    ppermute x1, starting transfers between devices, local(): first = lax.ppermute(to_first, axes, lat_first)  1.92 us
    ppermute x1, waiting for transfers between devices, local(): first = lax.ppermute(to_first, axes, lat_first)  1.37 us
    select_n x1, other arithmetic, half(): jnp.where(even, lax.slice_in_dim(value, 0, HALO, axis=dim), lax.slice_in_...  1.04 us
  transfers between devices with their start and end apart: 5, of which 2 were waited for; matrix products, arithmetic and copies ran while one was open for 0% of the time, Pallas kernels for 11%

profile of v5, /device:TPU:27, one launch (start us, length us, event | category | flops | bytes accessed | tf_op | source)
XLA Modules:
  0.0 32.7 jit_solution(9651434434939140020)
XLA Ops:
  0.0 0.0 copy-start.2
  0.0 0.0 copy-start.1
  0.0 1.0 %slice_select_fusion = f32[4,10,8,128]{3,2,1,0:T(8,128)S(1)} fusion(f32[4,10,16,128]{3,2,1,0:T(8,128)} %fields_ref.7, pred[]{:T(512)S(6)} %eq.5), kind=kLoop, calls=%fused_computation.1 | loop fusion | flops 40960 | bytes 491521 | tf_op jit(solution)/shard_map/jit(_where)/select_n | solution.py:415
  1.0 0.0 copy-done.2
  1.1 0.0 copy-start
  1.1 0.0 copy-done.1
  1.1 0.1 pad.3.clone
  1.2 0.1 maximum_maximum_fusion
  1.3 12.7 %collective-permute-start = (f32[43,8,128]{2,1,0:T(8,128)S(1)}, f32[43,8,128]{2,1,0:T(8,128)S(1)}, u32[]{:S(2)}, u32[]{:S(2)}) collective-permute-start(f32[43,8,128]{2,1,0:T(8,128)S(1)} %maximum_maximum_fusion), channel_id=1, source_target_pairs={{1,2},{2,1},{3,4},{4,3},{5,6},{6,5},{7,8},{8,7},{9,10},{10,9},{11,... | collective-permute-start | bytes 528392 | tf_op jit(solution)/shard_map/ppermute | solution.py:428
  14.0 0.0 copy-done
  14.1 1.9 %collective-permute-start.1 = (f32[42,8,128]{2,1,0:T(8,128)S(1)}, f32[42,8,128]{2,1,0:T(8,128)S(1)}, u32[]{:S(2)}, u32[]{:S(2)}) collective-permute-start(f32[42,8,128]{2,1,0:T(8,128)S(1)} %shard_map.37), channel_id=1, source_target_pairs={{0,1},{1,0},{2,3},{3,2},{4,5},{5,4},{6,7},{7,6},{8,9},{9,8},{10,11... | collective-permute-start | bytes 516104 | tf_op jit(solution)/shard_map/ppermute | solution.py:430
  16.0 1.4 %collective-permute-done.1.first_ref = f32[42,8,128]{2,1,0:T(8,128)S(1)} collective-permute-done((f32[42,8,128]{2,1,0:T(8,128)S(1)}, f32[42,8,128]{2,1,0:T(8,128)S(1)}, u32[]{:S(2)}, u32[]{:S(2)}) %collective-permute-start.1) | collective-permute-done | bytes 172064 | tf_op jit(solution)/shard_map/ppermute | solution.py:430
  17.4 0.4 %shard_map.38 = (f32[3,48,128]{2,1,0:T(8,128)S(1)}, f32[3,24,128]{2,1,0:T(8,128)S(1)}) custom-call(s32[1]{0:T(128)} %bitcast.lat_ref, s32[1]{0:T(128)} %bitcast.1.lon_ref, f32[4,10,16,128]{3,2,1,0:T(8,128)S(1)} %copy-done, f32[2,16,128]{2,1,0:T(8,128)S(1)} %pad_maximum_fusion.flat_ref, f32[42,8,128]{2,1,0:T(8,128)S(1)} %collective-permute-done.1.first_ref), custom_call_target="tpu_custom_call" | custom-call | flops 100000 | bytes 1000000 | tf_op jit(solution)/shard_map/pallas_call | solution.py:370
  17.7 2.4 %collective-permute-start.2 = (f32[3,48,128]{2,1,0:T(8,128)S(1)}, f32[3,48,128]{2,1,0:T(8,128)S(1)}, u32[]{:S(2)}, u32[]{:S(2)}) collective-permute-start(f32[3,48,128]{2,1,0:T(8,128)S(1)} %get-tuple-element.14.second_early_ref.sent_ref), channel_id=1, source_target_pairs={{15,511},{255,271},{271,255},{511,15}} | collective-permute-start | bytes 221192 | tf_op jit(solution)/shard_map/ppermute | solution.py:435
  20.1 2.4 %collective-permute-done.received_ref = f32[43,8,128]{2,1,0:T(8,128)S(1)} collective-permute-done((f32[43,8,128]{2,1,0:T(8,128)S(1)}, f32[43,8,128]{2,1,0:T(8,128)S(1)}, u32[]{:S(2)}, u32[]{:S(2)}) %collective-permute-start) | collective-permute-done | bytes 176160 | tf_op jit(solution)/shard_map/ppermute | solution.py:428
  22.5 0.3 shard_map.39
  22.8 0.7 %collective-permute-start.3 = (f32[3,32,128]{2,1,0:T(8,128)S(1)}, f32[3,32,128]{2,1,0:T(8,128)S(1)}, u32[]{:S(2)}, u32[]{:S(2)}) collective-permute-start(f32[3,32,128]{2,1,0:T(8,128)S(1)} %get-tuple-element.17), channel_id=1, source_target_pairs={{0,496},{1,497},{2,498},{3,499},{4,500},{5,501},{6,502},{7,503},{8... | collective-permute-start | bytes 147464 | tf_op jit(solution)/shard_map/ppermute | solution.py:440
  23.4 3.0 %collective-permute-start.4 = (f32[3,32,128]{2,1,0:T(8,128)S(1)}, f32[3,32,128]{2,1,0:T(8,128)S(1)}, u32[]{:S(2)}, u32[]{:S(2)}) collective-permute-start(f32[3,32,128]{2,1,0:T(8,128)S(1)} %get-tuple-element.18), channel_id=1, source_target_pairs={{0,16},{1,17},{2,18},{3,19},{4,20},{5,21},{6,22},{7,23},{8,24},{9,... | collective-permute-start | bytes 147464 | tf_op jit(solution)/shard_map/ppermute | solution.py:441
  26.4 2.9 %shard_map.40.block_ref = f32[4,10,16,128]{3,2,1,0:T(8,128)S(1)} custom-call(s32[1]{0:T(128)} %bitcast.lat_ref, f32[4,10,16,128]{3,2,1,0:T(8,128)S(1)} %copy-done, f32[2,16,128]{2,1,0:T(8,128)S(1)} %pad_maximum_fusion.flat_ref, f32[42,8,128]{2,1,0:T(8,128)S(1)} %get-tuple-element.16.second_ref, f32[42,8,128]{2,1,0:T(8,128)S(1)} %collective-permute-done.1.first_ref), custom_call_target="tpu_custom_call" | custom-call | flops 1000000000 | bytes 1000000 | tf_op jit(solution)/shard_map/pallas_call | solution.py:370
  29.4 0.0 collective-permute-done.3.second_side_ref
  29.4 0.0 collective-permute-done.4.first_side_ref
  29.4 0.0 collective-permute-done.2.early_ref
  29.4 3.3 %shard_map.41 = f32[4,10,16,128]{3,2,1,0:T(8,128)} custom-call(s32[1]{0:T(128)} %bitcast.lat_ref, s32[1]{0:T(128)} %bitcast.1.lon_ref, f32[4,10,16,128]{3,2,1,0:T(8,128)S(1)} %copy-done, f32[2,16,128]{2,1,0:T(8,128)S(1)} %pad_maximum_fusion.flat_ref, f32[42,8,128]{2,1,0:T(8,128)S(1)} %get-tuple-element.16.second_ref, ...), custom_call_target="tpu_custom_call" | custom-call | flops 100000000 | bytes 1000000 | tf_op jit(solution)/shard_map/pallas_call | solution.py:370
  (5 shorter events, 0.0 us)
Async XLA Ops:
  0.0 1.0 %copy-start.2 = (f32[16,128]{1,0:T(8,128)S(1)}, f32[16,128]{1,0:T(8,128)}, u32[]{:S(2)}) copy-start(f32[16,128]{1,0:T(8,128)} %param.6) | copy-start | bytes 24580
  0.0 1.1 %copy-start.1 = (s32[16,128]{1,0:T(8,128)S(1)}, s32[16,128]{1,0:T(8,128)}, u32[]{:S(2)}) copy-start(s32[16,128]{1,0:T(8,128)} %param.5) | copy-start | bytes 24580
  1.1 13.0 %copy-start = (f32[4,10,16,128]{3,2,1,0:T(8,128)S(1)}, f32[4,10,16,128]{3,2,1,0:T(8,128)}, u32[]{:S(2)}) copy-start(f32[4,10,16,128]{3,2,1,0:T(8,128)} %fields_ref.7) | copy-start | bytes 983044
  1.3 21.2 %collective-permute-start = (f32[43,8,128]{2,1,0:T(8,128)S(1)}, f32[43,8,128]{2,1,0:T(8,128)S(1)}, u32[]{:S(2)}, u32[]{:S(2)}) collective-permute-start(f32[43,8,128]{2,1,0:T(8,128)S(1)} %maximum_maximum_fusion), channel_id=1, source_target_pairs={{1,2},{2,1},{3,4},{4,3},{5,6},{6,5},{7,8},{8,7},{9,10},{10,9},{11,... | collective-permute-start | bytes 528392 | tf_op jit(solution)/shard_map/ppermute | solution.py:428
  14.1 3.3 %collective-permute-start.1 = (f32[42,8,128]{2,1,0:T(8,128)S(1)}, f32[42,8,128]{2,1,0:T(8,128)S(1)}, u32[]{:S(2)}, u32[]{:S(2)}) collective-permute-start(f32[42,8,128]{2,1,0:T(8,128)S(1)} %shard_map.37), channel_id=1, source_target_pairs={{0,1},{1,0},{2,3},{3,2},{4,5},{5,4},{6,7},{7,6},{8,9},{9,8},{10,11... | collective-permute-start | bytes 516104 | tf_op jit(solution)/shard_map/ppermute | solution.py:430
  17.7 11.7 %collective-permute-start.2 = (f32[3,48,128]{2,1,0:T(8,128)S(1)}, f32[3,48,128]{2,1,0:T(8,128)S(1)}, u32[]{:S(2)}, u32[]{:S(2)}) collective-permute-start(f32[3,48,128]{2,1,0:T(8,128)S(1)} %get-tuple-element.14.second_early_ref.sent_ref), channel_id=1, source_target_pairs={{15,511},{255,271},{271,255},{511,15}} | collective-permute-start | bytes 221192 | tf_op jit(solution)/shard_map/ppermute | solution.py:435
  22.8 6.6 %collective-permute-start.3 = (f32[3,32,128]{2,1,0:T(8,128)S(1)}, f32[3,32,128]{2,1,0:T(8,128)S(1)}, u32[]{:S(2)}, u32[]{:S(2)}) collective-permute-start(f32[3,32,128]{2,1,0:T(8,128)S(1)} %get-tuple-element.17), channel_id=1, source_target_pairs={{0,496},{1,497},{2,498},{3,499},{4,500},{5,501},{6,502},{7,503},{8... | collective-permute-start | bytes 147464 | tf_op jit(solution)/shard_map/ppermute | solution.py:440
  23.4 6.0 %collective-permute-start.4 = (f32[3,32,128]{2,1,0:T(8,128)S(1)}, f32[3,32,128]{2,1,0:T(8,128)S(1)}, u32[]{:S(2)}, u32[]{:S(2)}) collective-permute-start(f32[3,32,128]{2,1,0:T(8,128)S(1)} %get-tuple-element.18), channel_id=1, source_target_pairs={{0,16},{1,17},{2,18},{3,19},{4,20},{5,21},{6,22},{7,23},{8,24},{9,... | collective-permute-start | bytes 147464 | tf_op jit(solution)/shard_map/ppermute | solution.py:441

commit v6 on v5

--- a/solution.py
+++ b/solution.py
@@ -107,21 +107,25 @@
     return tiles
 
 
-def pack_early_kernel(lat_ref, lon_ref, fields_ref, flat_ref, first_ref, second_side_ref, first_side_ref):
+def pack_own_kernel(lon_ref, fields_ref, flat_ref, second_own_ref, first_own_ref):
     read = plane_reader(fields_ref, flat_ref)
+    lon_even = lon_ref[0] % 2 == 0
+    for ref, shift in ((second_own_ref, jnp.where(lon_even, 0, HALO)), (first_own_ref, jnp.where(lon_even, HALO, 0))):
+        for group, tile in enumerate(side_tiles(ROWS, lambda plane: read(plane, 0, ROWS), shift)):
+            ref[group] = tile
+
+
+def pack_early_kernel(lat_ref, lon_ref, first_ref, second_own_ref, first_own_ref, second_side_ref, first_side_ref):
     lat_even, lon_even = lat_ref[0] % 2 == 0, lon_ref[0] % 2 == 0
-
-    def early(plane):
-        own, halo = read(plane, 0, ROWS), first_ref[plane]
-        top = jnp.where(lat_even, own[:HALO], halo)
-        middle = jnp.where(lat_even, own[HALO:], own[:HALO])
-        return jnp.concatenate([top, middle, jnp.where(lat_even, halo, own[HALO:])], axis=0)
-
-    for ref, shift in (
-        (second_side_ref, jnp.where(lon_even, 0, HALO)), (first_side_ref, jnp.where(lon_even, HALO, 0))
+    own_at = pl.multiple_of(jnp.where(lat_even, 0, HALO), HALO)
+    halo_at = pl.multiple_of(jnp.where(lat_even, ROWS, 0), HALO)
+    for ref, own_ref, shift in (
+        (second_side_ref, second_own_ref, jnp.where(lon_even, 0, HALO)),
+        (first_side_ref, first_own_ref, jnp.where(lon_even, HALO, 0)),
     ):
-        for group, tile in enumerate(side_tiles(EARLY, early, shift)):
-            ref[group, pl.ds(0, EARLY), :] = tile
+        for group, tile in enumerate(side_tiles(HALO, lambda plane: first_ref[plane], shift)):
+            ref[group, pl.ds(own_at, ROWS), :] = own_ref[group]
+            ref[group, pl.ds(halo_at, HALO), :] = tile
     for group in range(GROUPS):
         for row in range(EARLY, SPARE, 8):
             second_side_ref[group, pl.ds(row, 8), :] = jnp.zeros((8, LANES), jnp.float32)
@@ -428,9 +432,10 @@
     received = lax.ppermute(to_second, axes, lat_second)
     to_first = call(pack_first_kernel, rows_message, (), 10**5, 10**6, lat, fields, flat)
     first = lax.ppermute(to_first, axes, lat_first)
+    second_own, first_own = call(pack_own_kernel, (f32(GROUPS, ROWS, LANES),) * 2, (), 10**5, 10**6, lon, fields, flat)
     to_second_early, to_first_early = call(
         pack_early_kernel, (f32(GROUPS, SPARE, LANES), f32(GROUPS, EARLY, LANES)), (), 10**5, 10**6,
-        lat, lon, fields, flat, first,
+        lat, lon, first, second_own, first_own,
     )
     early = lax.ppermute(to_second_early, axes, lon_early)
     second, to_second_side, to_first_side = call(

time: 32.9 us -> 32.9 us (level)
    pallas_call x5 -> x6, Pallas kernels: 6.82 us -> 6.89 us  [call(): pl.pallas_call(kernel, out_shape=out_shape, in_specs=[pl.BlockSpec(memory...]
where the time goes in v6:
time: 32.9 us; the launch traced here: 32.7 us
  starting transfers between devices  20.7 us (63%)
  Pallas kernels  6.89 us (21%)
  waiting for transfers between devices  3.66 us (11%)
  other arithmetic  1.17 us (4%)
    ppermute x1, starting transfers between devices, local(): received = lax.ppermute(to_second, axes, lat_second)  12.7 us
    pallas_call x6, Pallas kernels, call(): pl.pallas_call(kernel, out_shape=out_shape, in_specs=[pl.BlockSpec(memory...  6.89 us
    ppermute x1, starting transfers between devices, local(): first_side = lax.ppermute(to_first_side, axes, lon_first)  3 us
    ppermute x1, waiting for transfers between devices, local(): received = lax.ppermute(to_second, axes, lat_second)  2.55 us
    ppermute x1, starting transfers between devices, local(): early = lax.ppermute(to_second_early, axes, lon_early)  2.4 us
    ppermute x1, starting transfers between devices, local(): first = lax.ppermute(to_first, axes, lat_first)  1.92 us
    ppermute x1, waiting for transfers between devices, local(): first = lax.ppermute(to_first, axes, lat_first)  1.1 us
    select_n x1, other arithmetic, half(): jnp.where(even, lax.slice_in_dim(value, 0, HALO, axis=dim), lax.slice_in_...  1.04 us
  transfers between devices with their start and end apart: 5, of which 2 were waited for; matrix products, arithmetic and copies ran while one was open for 0% of the time, Pallas kernels for 11%

profile of v6, /device:TPU:27, one launch (start us, length us, event | category | flops | bytes accessed | tf_op | source)
XLA Modules:
  0.0 32.7 jit_solution(5077907082978861472)
XLA Ops:
  0.0 0.0 copy-start.2
  0.0 0.0 copy-start.1
  0.0 1.0 %slice_select_fusion = f32[4,10,8,128]{3,2,1,0:T(8,128)S(1)} fusion(f32[4,10,16,128]{3,2,1,0:T(8,128)} %fields_ref.7, pred[]{:T(512)S(6)} %eq.5), kind=kLoop, calls=%fused_computation.1 | loop fusion | flops 40960 | bytes 491521 | tf_op jit(solution)/shard_map/jit(_where)/select_n | solution.py:419
  1.0 0.0 copy-done.2
  1.1 0.0 copy-start
  1.1 0.0 copy-done.1
  1.1 0.1 pad.3.clone
  1.2 0.1 maximum_maximum_fusion
  1.3 12.7 %collective-permute-start = (f32[43,8,128]{2,1,0:T(8,128)S(1)}, f32[43,8,128]{2,1,0:T(8,128)S(1)}, u32[]{:S(2)}, u32[]{:S(2)}) collective-permute-start(f32[43,8,128]{2,1,0:T(8,128)S(1)} %maximum_maximum_fusion), channel_id=1, source_target_pairs={{1,2},{2,1},{3,4},{4,3},{5,6},{6,5},{7,8},{8,7},{9,10},{10,9},{11,... | collective-permute-start | bytes 528392 | tf_op jit(solution)/shard_map/ppermute | solution.py:432
  14.0 0.0 copy-done
  14.1 1.9 %collective-permute-start.1 = (f32[42,8,128]{2,1,0:T(8,128)S(1)}, f32[42,8,128]{2,1,0:T(8,128)S(1)}, u32[]{:S(2)}, u32[]{:S(2)}) collective-permute-start(f32[42,8,128]{2,1,0:T(8,128)S(1)} %shard_map.37), channel_id=1, source_target_pairs={{0,1},{1,0},{2,3},{3,2},{4,5},{5,4},{6,7},{7,6},{8,9},{9,8},{10,11... | collective-permute-start | bytes 516104 | tf_op jit(solution)/shard_map/ppermute | solution.py:434
  16.0 0.3 shard_map.38
  16.2 1.1 %collective-permute-done.1.first_ref = f32[42,8,128]{2,1,0:T(8,128)S(1)} collective-permute-done((f32[42,8,128]{2,1,0:T(8,128)S(1)}, f32[42,8,128]{2,1,0:T(8,128)S(1)}, u32[]{:S(2)}, u32[]{:S(2)}) %collective-permute-start.1) | collective-permute-done | bytes 172064 | tf_op jit(solution)/shard_map/ppermute | solution.py:434
  17.4 0.2 shard_map.39
  17.5 2.4 %collective-permute-start.2 = (f32[3,48,128]{2,1,0:T(8,128)S(1)}, f32[3,48,128]{2,1,0:T(8,128)S(1)}, u32[]{:S(2)}, u32[]{:S(2)}) collective-permute-start(f32[3,48,128]{2,1,0:T(8,128)S(1)} %get-tuple-element.18.second_early_ref.sent_ref), channel_id=1, source_target_pairs={{15,511},{255,271},{271,255},{511,15}} | collective-permute-start | bytes 221192 | tf_op jit(solution)/shard_map/ppermute | solution.py:440
  19.9 2.5 %collective-permute-done.received_ref = f32[43,8,128]{2,1,0:T(8,128)S(1)} collective-permute-done((f32[43,8,128]{2,1,0:T(8,128)S(1)}, f32[43,8,128]{2,1,0:T(8,128)S(1)}, u32[]{:S(2)}, u32[]{:S(2)}) %collective-permute-start) | collective-permute-done | bytes 176160 | tf_op jit(solution)/shard_map/ppermute | solution.py:432
  22.5 0.3 shard_map.40
  22.8 0.7 %collective-permute-start.3 = (f32[3,32,128]{2,1,0:T(8,128)S(1)}, f32[3,32,128]{2,1,0:T(8,128)S(1)}, u32[]{:S(2)}, u32[]{:S(2)}) collective-permute-start(f32[3,32,128]{2,1,0:T(8,128)S(1)} %get-tuple-element.21), channel_id=1, source_target_pairs={{0,496},{1,497},{2,498},{3,499},{4,500},{5,501},{6,502},{7,503},{8... | collective-permute-start | bytes 147464 | tf_op jit(solution)/shard_map/ppermute | solution.py:445
  23.4 3.0 %collective-permute-start.4 = (f32[3,32,128]{2,1,0:T(8,128)S(1)}, f32[3,32,128]{2,1,0:T(8,128)S(1)}, u32[]{:S(2)}, u32[]{:S(2)}) collective-permute-start(f32[3,32,128]{2,1,0:T(8,128)S(1)} %get-tuple-element.22), channel_id=1, source_target_pairs={{0,16},{1,17},{2,18},{3,19},{4,20},{5,21},{6,22},{7,23},{8,24},{9,... | collective-permute-start | bytes 147464 | tf_op jit(solution)/shard_map/ppermute | solution.py:446
  26.4 2.9 %shard_map.41.block_ref = f32[4,10,16,128]{3,2,1,0:T(8,128)S(1)} custom-call(s32[1]{0:T(128)} %bitcast.lat_ref, f32[4,10,16,128]{3,2,1,0:T(8,128)S(1)} %copy-done, f32[2,16,128]{2,1,0:T(8,128)S(1)} %pad_maximum_fusion.flat_ref, f32[42,8,128]{2,1,0:T(8,128)S(1)} %get-tuple-element.20.second_ref, f32[42,8,128]{2,1,0:T(8,128)S(1)} %collective-permute-done.1.first_ref), custom_call_target="tpu_custom_call" | custom-call | flops 1000000000 | bytes 1000000 | tf_op jit(solution)/shard_map/pallas_call | solution.py:374
  29.4 0.0 collective-permute-done.3.second_side_ref
  29.4 0.0 collective-permute-done.4.first_side_ref
  29.4 0.0 collective-permute-done.2.early_ref
  29.4 3.3 %shard_map.42 = f32[4,10,16,128]{3,2,1,0:T(8,128)} custom-call(s32[1]{0:T(128)} %bitcast.lat_ref, s32[1]{0:T(128)} %bitcast.1.lon_ref, f32[4,10,16,128]{3,2,1,0:T(8,128)S(1)} %copy-done, f32[2,16,128]{2,1,0:T(8,128)S(1)} %pad_maximum_fusion.flat_ref, f32[42,8,128]{2,1,0:T(8,128)S(1)} %get-tuple-element.20.second_ref, ...), custom_call_target="tpu_custom_call" | custom-call | flops 100000000 | bytes 1000000 | tf_op jit(solution)/shard_map/pallas_call | solution.py:374
  (5 shorter events, 0.0 us)
Async XLA Ops:
  0.0 1.0 %copy-start.2 = (f32[16,128]{1,0:T(8,128)S(1)}, f32[16,128]{1,0:T(8,128)}, u32[]{:S(2)}) copy-start(f32[16,128]{1,0:T(8,128)} %param.6) | copy-start | bytes 24580
  0.0 1.1 %copy-start.1 = (s32[16,128]{1,0:T(8,128)S(1)}, s32[16,128]{1,0:T(8,128)}, u32[]{:S(2)}) copy-start(s32[16,128]{1,0:T(8,128)} %param.5) | copy-start | bytes 24580
  1.1 13.0 %copy-start = (f32[4,10,16,128]{3,2,1,0:T(8,128)S(1)}, f32[4,10,16,128]{3,2,1,0:T(8,128)}, u32[]{:S(2)}) copy-start(f32[4,10,16,128]{3,2,1,0:T(8,128)} %fields_ref.7) | copy-start | bytes 983044
  1.3 21.2 %collective-permute-start = (f32[43,8,128]{2,1,0:T(8,128)S(1)}, f32[43,8,128]{2,1,0:T(8,128)S(1)}, u32[]{:S(2)}, u32[]{:S(2)}) collective-permute-start(f32[43,8,128]{2,1,0:T(8,128)S(1)} %maximum_maximum_fusion), channel_id=1, source_target_pairs={{1,2},{2,1},{3,4},{4,3},{5,6},{6,5},{7,8},{8,7},{9,10},{10,9},{11,... | collective-permute-start | bytes 528392 | tf_op jit(solution)/shard_map/ppermute | solution.py:432
  14.1 3.3 %collective-permute-start.1 = (f32[42,8,128]{2,1,0:T(8,128)S(1)}, f32[42,8,128]{2,1,0:T(8,128)S(1)}, u32[]{:S(2)}, u32[]{:S(2)}) collective-permute-start(f32[42,8,128]{2,1,0:T(8,128)S(1)} %shard_map.37), channel_id=1, source_target_pairs={{0,1},{1,0},{2,3},{3,2},{4,5},{5,4},{6,7},{7,6},{8,9},{9,8},{10,11... | collective-permute-start | bytes 516104 | tf_op jit(solution)/shard_map/ppermute | solution.py:434
  17.5 11.9 %collective-permute-start.2 = (f32[3,48,128]{2,1,0:T(8,128)S(1)}, f32[3,48,128]{2,1,0:T(8,128)S(1)}, u32[]{:S(2)}, u32[]{:S(2)}) collective-permute-start(f32[3,48,128]{2,1,0:T(8,128)S(1)} %get-tuple-element.18.second_early_ref.sent_ref), channel_id=1, source_target_pairs={{15,511},{255,271},{271,255},{511,15}} | collective-permute-start | bytes 221192 | tf_op jit(solution)/shard_map/ppermute | solution.py:440
  22.8 6.6 %collective-permute-start.3 = (f32[3,32,128]{2,1,0:T(8,128)S(1)}, f32[3,32,128]{2,1,0:T(8,128)S(1)}, u32[]{:S(2)}, u32[]{:S(2)}) collective-permute-start(f32[3,32,128]{2,1,0:T(8,128)S(1)} %get-tuple-element.21), channel_id=1, source_target_pairs={{0,496},{1,497},{2,498},{3,499},{4,500},{5,501},{6,502},{7,503},{8... | collective-permute-start | bytes 147464 | tf_op jit(solution)/shard_map/ppermute | solution.py:445
  23.4 6.0 %collective-permute-start.4 = (f32[3,32,128]{2,1,0:T(8,128)S(1)}, f32[3,32,128]{2,1,0:T(8,128)S(1)}, u32[]{:S(2)}, u32[]{:S(2)}) collective-permute-start(f32[3,32,128]{2,1,0:T(8,128)S(1)} %get-tuple-element.22), channel_id=1, source_target_pairs={{0,16},{1,17},{2,18},{3,19},{4,20},{5,21},{6,22},{7,23},{8,24},{9,... | collective-permute-start | bytes 147464 | tf_op jit(solution)/shard_map/ppermute | solution.py:446
